TPU v7x, 32 devices: a whole 2x2x4 slice. The times are simulated.
32 devices in a mesh: ctx: 2 (over y), exp: 16 (over z, x, core).
Axes of the slice: x: 2, y: 2, z: 4, core: 2. Of those that a mesh axis runs over, the one named last changes fastest.
Arguments:
- inputs: bfloat16 [1536, 1024], P('exp', 'ctx'), may hold values from -6 to 6
- pre_act: bfloat16 [1536, 1024], P('exp', 'ctx'), may hold values from -6 to 6
- grad_out: bfloat16 [1536, 1024], P('exp', 'ctx'), may hold values from -6 to 6
- conv_weight: bfloat16 [5, 1536, 1536], P(None, 'exp', 'ctx'), may hold values from -0.0625 to 0.0625
- expert_ids: int32 [1024, 2], P('ctx'), may hold values from 0 to 15, as said below
- gate_values: float32 [1024, 2], P('ctx'), may hold values from 0.1 to 0.9
- expert_in: bfloat16 [16, 1536, 3072], P('exp', None, 'ctx'), may hold values from -0.15625 to 0.15625
- expert_out: bfloat16 [16, 3072, 1536], P('exp', 'ctx'), may hold values from -0.109375 to 0.109375
Outputs:
- grad_inputs: bfloat16 [1536, 1024], P('exp', 'ctx')
- grad_conv: float32 [5, 1536, 1536], P(None, 'exp', 'ctx')
- grad_expert_in: bfloat16 [16, 1536, 3072], P('exp', None, 'ctx')
- grad_expert_out: bfloat16 [16, 3072, 1536], P('exp', 'ctx')
Inputs may be any that keep to these rules, and one draw needn't show every extreme that they name: `expert_ids`: the 2 ids of a bin differ. In each aligned block of 512 bins (the bins of one index of ctx) no expert is named more than 128 times, and one expert, the same in every block, is named exactly 128 times in each block.
All inputs are finite; a program needn't handle non-finite values.
Results may differ from a plain program's by a relative error of at most 0.009.
Values may be sent and summed in bfloat16 or wider, within the bound.
A program may use at most 128 MiB of HBM per device.

v0:
```python
import jax
import jax.numpy as jnp
from jax import lax
from jax.sharding import PartitionSpec as P


def with_halo(cells, sides, width):
    for axis, dim in sides:
        count = lax.axis_size(axis)
        ends = count - 1
        head = lax.slice_in_dim(cells, 0, width, axis=dim)
        tail = lax.slice_in_dim(cells, cells.shape[dim] - width, cells.shape[dim], axis=dim)
        cells = jnp.concatenate(
            [
                lax.ppermute(tail, axis, [(i, (i + 1) % count) for i in range(ends)]),
                cells,
                lax.ppermute(head, axis, [((i + 1) % count, i) for i in range(ends)]),
            ],
            axis=dim,
        )
    return cells


def gelu_value(values):
    factor = 0.7978845608028654
    return 0.5 * values * (1.0 + jnp.tanh(factor * (values + 0.044715 * values * values * values)))


def gelu_slope(values):
    factor = 0.7978845608028654
    tangent = jnp.tanh(factor * (values + 0.044715 * values * values * values))
    return 0.5 * (1.0 + tangent) + 0.5 * values * (1.0 - tangent * tangent) * factor * (
        1.0 + 0.134145 * values * values
    )


def turned(left, right, dims):
    return lax.dot_general(
        left.astype(jnp.float32),
        right.astype(jnp.float32),
        (dims, ((), ())),
        preferred_element_type=jnp.float32,
    )


def expert_pass(w_first, w_second, rows_in, rows_grad):
    hidden = turned(w_first, rows_in, ((0,), (0,)))
    squashed = gelu_value(hidden).astype(jnp.bfloat16)
    grad_second = turned(squashed, rows_grad, ((1,), (1,)))
    grad_hidden = jnp.dot(w_second, rows_grad, preferred_element_type=jnp.float32)
    grad_pre = (grad_hidden * gelu_slope(hidden)).astype(jnp.bfloat16)
    grad_first = turned(rows_in, grad_pre, ((1,), (1,)))
    grad_rows = jnp.dot(w_first, grad_pre, preferred_element_type=jnp.float32)
    return (grad_first, grad_second, grad_rows)


def local(inputs, pre_act, grad_out, conv_weight, expert_ids, gate_values, expert_in, expert_out):
    channels, bins_local = inputs.shape
    experts = lax.axis_size("exp")
    groups = lax.axis_size("ctx")
    capacity = 4 * bins_local // experts
    model_width = channels * experts
    kernel = conv_weight.shape[0]
    margin = kernel // 2
    pre_float = pre_act.astype(jnp.float32)
    activated = (inputs.astype(jnp.float32) + gelu_value(pre_float)).astype(jnp.bfloat16)
    grad_float = grad_out.astype(jnp.float32)
    flat_ids = expert_ids.reshape(-1)
    onehot = (flat_ids[:, None] == jnp.arange(experts, dtype=jnp.int32)[None, :]).astype(jnp.int32)
    slot_index = jnp.sum(onehot * jnp.cumsum(onehot, axis=0), axis=1) - 1
    targets = flat_ids * capacity + slot_index
    owners = jnp.arange(flat_ids.shape[0], dtype=jnp.int32) // expert_ids.shape[1]
    row_table = jnp.full((experts * capacity,), bins_local, jnp.int32).at[targets].set(owners)
    gate_table = (
        jnp.zeros((experts * capacity,), jnp.float32).at[targets].set(gate_values.reshape(-1))
    )
    act_pad = jnp.concatenate([activated, jnp.zeros((channels, 1), jnp.bfloat16)], axis=1)
    grad_pad = jnp.concatenate([grad_float, jnp.zeros((channels, 1), jnp.float32)], axis=1)
    send_rows = act_pad[:, row_table].reshape(channels, experts, capacity)
    send_grad = (
        (grad_pad[:, row_table] * gate_table[None, :])
        .astype(jnp.bfloat16)
        .reshape(channels, experts, capacity)
    )
    weight_first = expert_in[0]
    weight_second = expert_out[0]
    total_rows = groups * capacity
    copied = (
        lax.all_gather(send_rows, "ctx", axis=2, tiled=True),
        lax.all_gather(send_grad, "ctx", axis=2, tiled=True),
    )
    arrived = (
        lax.all_to_all(copied[0], "exp", split_axis=1, concat_axis=0, tiled=True),
        lax.all_to_all(copied[1], "exp", split_axis=1, concat_axis=0, tiled=True),
    )
    part_in, part_out, part_rows = expert_pass(
        weight_first, weight_second, arrived[0][:, 0, :], arrived[1][:, 0, :]
    )
    rows_back = part_rows
    sum_first, sum_second, rows_back = (part_in, part_out, rows_back)
    moved_back = lax.all_to_all(
        rows_back.reshape(model_width, 1, total_rows),
        "exp",
        split_axis=0,
        concat_axis=1,
        tiled=True,
    )
    returned = lax.psum_scatter(moved_back, "ctx", scatter_dimension=2, tiled=True).astype(
        jnp.bfloat16
    )
    back_flat = returned.reshape(channels, experts * capacity).astype(jnp.float32)
    per_bin = targets.reshape(bins_local, -1)
    grad_total = grad_float
    for column in range(per_bin.shape[1]):
        grad_total = grad_total + back_flat[:, per_bin[:, column]]
    grad_pre_conv = (grad_total * gelu_slope(pre_float)).astype(jnp.bfloat16)
    full_weight = lax.all_gather(conv_weight, "ctx", axis=2, tiled=True)
    rim_inputs = with_halo(inputs, (("ctx", 1),), margin)
    gathered = lax.all_gather(grad_pre_conv, "exp", axis=0, tiled=True)
    rim_grad = with_halo(gathered, (("ctx", 1),), margin)
    conv_back = jnp.zeros((channels, bins_local), jnp.float32)
    tap_grads = []
    for offset in range(kernel):
        lower = 2 * margin - offset
        weight_cols = full_weight[offset]
        conv_back = conv_back + jnp.dot(
            weight_cols, rim_grad[:, lower : lower + bins_local], preferred_element_type=jnp.float32
        )
        tap_grads.append(
            turned(
                rim_inputs[:, offset : offset + bins_local],
                rim_grad[:, margin : margin + bins_local],
                ((1,), (1,)),
            )
        )
    conv_grad = jnp.stack(tap_grads)
    conv_back, conv_grad = (conv_back, conv_grad)
    grad_inputs = (grad_total + conv_back).astype(jnp.bfloat16)
    grad_conv = lax.psum_scatter(
        conv_grad.astype(jnp.bfloat16), "ctx", scatter_dimension=2, tiled=True
    ).astype(jnp.float32)
    return (
        grad_inputs,
        grad_conv,
        sum_first.astype(jnp.bfloat16)[None],
        sum_second.astype(jnp.bfloat16)[None],
    )


def solution(mesh):
    placed = (
        P("exp", "ctx"),
        P("exp", "ctx"),
        P("exp", "ctx"),
        P(None, "exp", "ctx"),
        P("ctx", None),
        P("ctx", None),
        P("exp", None, "ctx"),
        P("exp", "ctx", None),
    )
    return jax.shard_map(
        local,
        mesh=mesh,
        in_specs=placed,
        out_specs=(
            P("exp", "ctx"),
            P(None, "exp", "ctx"),
            P("exp", None, "ctx"),
            P("exp", "ctx", None),
        ),
        check_vma=False,
    )
```

profile of v0, /device:TPU:0, one launch (start us, length us, event | category | flops | bytes accessed | tf_op | source)
XLA Modules:
  0.0 288.9 jit_solution(6828851017552488800)
XLA Ops:
  7.2 0.9 copy.47
  8.1 0.2 eq.29
  8.2 0.2 eq.25
  8.4 4.5 %reduce-window.6 = s32[16,8,128]{2,1,0:T(8,128)S(1)} reduce-window(s32[16,8,128]{2,1,0:T(8,128)S(1)} %fusion.94, s32[]{:T(128)} %constant.17.clone.1), window={size=1x1x128 pad=0_0x0_0x127_0}, to_apply=%region_0.0 | reduce-window | flops 2080768 | bytes 131076 | tf_op jit(solution)/shard_map/reduce-window
  13.0 0.1 copy.50
  13.4 0.2 sub.24
  13.6 0.2 mul.133
  13.8 4.3 %scatter_custom_fusion = s32[2048]{0:T(1024)S(1)} fusion(s32[1024]{0:T(1024)S(1)} %bitcast.156, s32[1024]{0:T(1024)S(1)} %add_select_fusion, s32[]{:T(128)} %constant.15.clone.1), kind=kCustom, calls=%fused_computation.131 | custom fusion | bytes 8196 | tf_op jit(solution)/shard_map/scatter | solution.py:73
  18.3 0.1 copy.63
  18.5 6.2 %gather_fusion.1 = bf16[2048,96]{1,0:T(8,128)(2,1)S(1)} fusion(bf16[96,513]{0,1:T(8,128)(2,1)S(1)} %concatenate.25.clone, s32[2048]{0:T(1024)S(1)} %fusion.95), kind=kCustom, calls=%fused_computation.1 | custom fusion | bytes 794624 | tf_op jit(solution)/shard_map/gather | solution.py:79
  24.7 0.3 copy.56
  24.9 13.0 %all_gather.13 = bf16[96,16,256]{2,0,1:T(8,128)(2,1)} all-gather(bf16[96,16,128]{2,0,1:T(8,128)(2,1)S(1)} %copy.56), channel_id=1, replica_groups=mesh['ctx'=2,'exp'=16] {'ctx'}, dimensions={2}, use_global_device_ids=true | all-gather | bytes 1179648 | tf_op jit(solution)/shard_map/all_gather | solution.py:89
  37.9 6.2 %all-to-all-start.1 = ((bf16[96,16,256]{2,0,1:T(8,128)(2,1)}), bf16[96,16,256]{2,0,1:T(8,128)(2,1)S(1)}, u32[]{:S(2)}, u32[]{:S(2)}) async-start(bf16[96,16,256]{2,0,1:T(8,128)(2,1)} %all_gather.13), calls=%async_computation.1 | async-start | bytes 1572864 | tf_op jit(solution)/shard_map/all_to_all | solution.py:93
  44.2 5.5 %gather_fusion = f32[2048,96]{1,0:T(8,128)S(1)} fusion(f32[96,513]{0,1:T(8,128)S(1)} %concatenate.24.clone, s32[2048]{0:T(1024)S(1)} %fusion.95), kind=kCustom, calls=%fused_computation | custom fusion | bytes 1581056 | tf_op jit(solution)/shard_map/gather | solution.py:81
  49.7 0.3 copy.54
  50.0 0.3 copy-done.12
  50.4 0.1 copy.53
  50.5 0.2 reshape.134
  50.7 4.3 %scatter_custom_fusion.1 = f32[2048]{0:T(1024)S(1)} fusion(s32[1024]{0:T(1024)S(1)} %bitcast.157, f32[1024]{0:T(1024)S(1)} %reshape.134, f32[]{:T(128)} %constant.14.clone.1), kind=kCustom, calls=%fused_computation.129 | custom fusion | bytes 8196 | tf_op jit(solution)/shard_map/scatter | solution.py:75
  55.1 12.2 %all_gather.12 = bf16[96,16,256]{2,0,1:T(8,128)(2,1)} all-gather(bf16[96,16,128]{2,0,1:T(8,128)(2,1)S(1)} %multiply_convert_fusion.2), channel_id=1, replica_groups=mesh['ctx'=2,'exp'=16] {'ctx'}, dimensions={2}, use_global_device_ids=true | all-gather | bytes 1179648 | tf_op jit(solution)/shard_map/all_gather | solution.py:90
  67.3 5.7 %all-to-all-start = ((bf16[96,16,256]{2,0,1:T(8,128)(2,1)}), bf16[96,16,256]{2,0,1:T(8,128)(2,1)S(1)}, u32[]{:S(2)}, u32[]{:S(2)}) async-start(bf16[96,16,256]{2,0,1:T(8,128)(2,1)} %all_gather.12), calls=%async_computation | async-start | bytes 1572864 | tf_op jit(solution)/shard_map/all_to_all | solution.py:94
  73.1 4.9 %fusion.14 = f32[1536,256]{0,1:T(8,128)} fusion(bf16[1536,256]{1,0:T(8,128)(2,1)S(1)} %bitcast.148, bf16[1,1536,1536]{2,1,0:T(8,128)(2,1)} %param.14), kind=kOutput, calls=%fused_computation.18 | convolution fusion | flops 1207959552 | bytes 7077888 | tf_op jit(solution)/shard_map/dot_general | solution.py:38
  78.0 13.8 %all-to-all-done = bf16[96,16,256]{2,0,1:T(8,128)(2,1)S(1)} async-done(((bf16[96,16,256]{2,0,1:T(8,128)(2,1)}), bf16[96,16,256]{2,0,1:T(8,128)(2,1)S(1)}, u32[]{:S(2)}, u32[]{:S(2)}) %all-to-all-start) | async-done | bytes 786464 | tf_op jit(solution)/shard_map/all_to_all | solution.py:94
  91.8 5.1 %fusion.20 = bf16[1536,256]{0,1:T(8,128)(2,1)S(1)} fusion(bf16[1536,256]{1,0:T(8,128)(2,1)S(1)} %bitcast.150, bf16[1,1536,1536]{2,1,0:T(8,128)(2,1)} %param.15, f32[1536,256]{0,1:T(8,128)} %fusion.14), kind=kOutput, calls=%fused_computation.20 | convolution fusion | flops 1215430656 | bytes 7864320 | tf_op jit(solution)/shard_map/dot_general | solution.py:50
  96.9 0.9 copy-done.13
  97.8 4.9 %fusion.17 = f32[1536,1,256]{0,2,1:T(8,128)} fusion(bf16[1536,256]{0,1:T(8,128)(2,1)S(1)} %fusion.20, bf16[1,1536,1536]{2,1,0:T(8,128)(2,1)} %param.14), kind=kOutput, calls=%fused_computation.19 | convolution fusion | flops 1207959552 | bytes 7077888 | tf_op jit(solution)/shard_map/dot_general | solution.py:53
  102.7 3.6 %copy.57 = f32[1536,1,256]{2,1,0:T(1,128)S(1)} copy(f32[1536,1,256]{0,2,1:T(8,128)} %fusion.17) | data formatting | bytes 3145728 | tf_op jit(solution)/shard_map/reshape | solution.py:102
  106.3 41.4 %all_to_all.48 = f32[1536,1,256]{2,1,0:T(1,128)S(1)} all-to-all(f32[1536,1,256]{2,1,0:T(1,128)S(1)} %copy.57), channel_id=1, replica_groups=mesh['ctx'=2,'exp'=16] {'exp'}, dimensions={0} | all-to-all | bytes 3145728 | tf_op jit(solution)/shard_map/all_to_all | solution.py:101
  147.6 1.2 copy.61
  149.0 0.3 fusion.73
  149.3 26.2 %reduce-scatter.3.cloned.1.call-done = f32[96,16,128]{2,0,1:T(8,128)} async-done(((f32[96,16,256]{2,0,1:T(8,128)}), f32[96,16,128]{2,0,1:T(8,128)}) %reduce-scatter.3.cloned.1.call-update) | async-done | bytes 786448 | tf_op jit(solution)/shard_map/reduce_scatter | solution.py:108
  175.5 1.2 convert_convert_fusion
  176.7 0.3 copy.58
  177.0 1.0 gather_fusion.2
  178.1 0.1 copy.59
  178.2 1.0 gather_fusion.3
  179.3 0.1 copy.60
  179.4 0.8 fusion.83
  180.4 2.2 collective-permute-start.2
  182.6 1.3 collective-permute-start.3
  183.9 0.2 reduce-scatter.5.cloned.1.call-start
  184.2 4.1 %collective-permute-done.3 = bf16[96,2]{1,0:T(8,128)(2,1)S(1)} collective-permute-done((bf16[96,2]{1,0:T(8,128)(2,1)S(1)}, bf16[96,2]{1,0:T(8,128)(2,1)S(1)}, u32[]{:S(2)}, u32[]{:S(2)}) %collective-permute-start.3) | collective-permute-done | bytes 416 | tf_op jit(solution)/shard_map/ppermute | solution.py:17
  188.3 31.7 %all-gather.3.cloned.1.call-done = bf16[1536,512]{1,0:T(8,128)(2,1)} async-done(((bf16[96,512]{1,0:T(8,128)(2,1)}), bf16[1536,512]{1,0:T(8,128)(2,1)}) %all-gather.3.cloned.1.call-update) | async-done | bytes 1572880 | tf_op jit(solution)/shard_map/all_gather | solution.py:119
  220.1 2.9 fusion.24
  222.9 1.3 fusion.26
  224.3 1.3 fusion.28
  225.6 1.3 fusion.30
  226.9 1.3 fusion.32
  228.3 4.9 %fusion = bf16[1,1536,1536]{2,1,0:T(8,128)(2,1)} fusion(bf16[1536,256]{1,0:T(8,128)(2,1)S(1)} %bitcast.149, bf16[1536,256]{0,1:T(8,128)(2,1)} %copy-done.13), kind=kOutput, calls=%fused_computation.8 | convolution fusion | flops 1210318848 | bytes 6291456 | tf_op jit(solution)/shard_map/dot_general | solution.py:38
  233.3 3.9 %fusion.1 = bf16[1,1536,1536]{2,1,0:T(8,128)(2,1)} fusion(bf16[1536,256]{1,0:T(8,128)(2,1)S(1)} %bitcast.151, f32[1536,256]{0,1:T(8,128)S(1)} %copy-done.14), kind=kOutput, calls=%fused_computation.9 | convolution fusion | flops 1213857792 | bytes 7077888 | tf_op jit(solution)/shard_map/dot_general | solution.py:38
  237.1 1.1 fusion.112
  238.2 1.3 collective-permute-start
  239.5 6.0 %collective-permute-start.1 = (bf16[1536,2]{1,0:T(8,128)(2,1)}, bf16[1536,2]{1,0:T(8,128)(2,1)}, u32[]{:S(2)}, u32[]{:S(2)}) collective-permute-start(bf16[1536,2]{1,0:T(8,128)(2,1)} %get-tuple-element.7), channel_id=1, source_target_pairs={{0,16},{1,17},{2,18},{3,19},{4,20},{5,21},{6,22},{7,23},{8,24},{9,... | collective-permute-start | bytes 18440 | tf_op jit(solution)/shard_map/ppermute | solution.py:15
  245.6 4.5 %all-gather.5.cloned.1.call-done = bf16[5,96,1536]{2,1,0:T(8,128)(2,1)} async-done(((bf16[5,96,768]{2,1,0:T(8,128)(2,1)}), bf16[5,96,1536]{2,1,0:T(8,128)(2,1)}) %all-gather.5.cloned.1.call-update) | async-done | bytes 1474576 | tf_op jit(solution)/shard_map/all_gather | solution.py:117
  250.1 1.5 fusion.72
  251.5 2.0 collective-permute-done.1
  253.6 1.7 fusion.39
  255.3 1.1 constant_dynamic-update-slice_fusion
  256.4 0.6 fusion.41
  257.1 0.6 fusion.62
  257.7 0.2 copy-done.5
  258.1 2.4 fusion.65
  260.5 19.5 %reduce-scatter.5.cloned.1.call-done = bf16[5,96,768]{2,1,0:T(8,128)(2,1)} async-done(((bf16[5,96,1536]{2,1,0:T(8,128)(2,1)}), bf16[5,96,768]{2,1,0:T(8,128)(2,1)}) %reduce-scatter.5.cloned.1.call-update) | async-done | bytes 737296 | tf_op jit(solution)/shard_map/reduce_scatter | solution.py:139
  280.0 2.3 convert_element_type.80
  (59 shorter events, 1.3 us)
Async XLA Ops:
  7.2 11.0 %copy-start.1 = (bf16[96,512]{1,0:T(8,128)(2,1)S(1)}, bf16[96,512]{1,0:T(8,128)(2,1)}, u32[]{:S(2)}) copy-start(bf16[96,512]{1,0:T(8,128)(2,1)} %param.8) | copy-start | bytes 294916
  7.2 11.0 %copy-start.8 = (bf16[96,512]{1,0:T(8,128)(2,1)S(1)}, bf16[96,512]{1,0:T(8,128)(2,1)}, u32[]{:S(2)}) copy-start(bf16[96,512]{1,0:T(8,128)(2,1)} %param.9) | copy-start | bytes 294916
  24.9 19.2 %copy-start.9 = (bf16[96,512]{1,0:T(8,128)(2,1)S(1)}, bf16[96,512]{1,0:T(8,128)(2,1)}, u32[]{:S(2)}) copy-start(bf16[96,512]{1,0:T(8,128)(2,1)} %param.10) | copy-start | bytes 294916
  37.9 29.5 %all-to-all-start.1 = ((bf16[96,16,256]{2,0,1:T(8,128)(2,1)}), bf16[96,16,256]{2,0,1:T(8,128)(2,1)S(1)}, u32[]{:S(2)}, u32[]{:S(2)}) async-start(bf16[96,16,256]{2,0,1:T(8,128)(2,1)} %all_gather.13), calls=%async_computation.1 | async-start | bytes 1572864 | tf_op jit(solution)/shard_map/all_to_all | solution.py:93
  49.7 0.7 copy-start.12
  67.3 24.4 %all-to-all-start = ((bf16[96,16,256]{2,0,1:T(8,128)(2,1)}), bf16[96,16,256]{2,0,1:T(8,128)(2,1)S(1)}, u32[]{:S(2)}, u32[]{:S(2)}) async-start(bf16[96,16,256]{2,0,1:T(8,128)(2,1)} %all_gather.12), calls=%async_computation | async-start | bytes 1572864 | tf_op jit(solution)/shard_map/all_to_all | solution.py:94
  73.1 102.4 %reduce-scatter.3.cloned.1.call-start = ((), (), s32[]{:S(2)}) async-start(), calls=%async_computation.5 | async-start | bytes 2359296 | tf_op jit(solution)/shard_map/reduce_scatter | solution.py:108
  91.8 5.1 %copy-start.2 = (bf16[96,16,256]{2,0,1:T(8,128)(2,1)}, bf16[96,16,256]{2,0,1:T(8,128)(2,1)S(1)}, u32[]{:S(2)}) copy-start(bf16[96,16,256]{2,0,1:T(8,128)(2,1)S(1)} %all-to-all-done) | copy-start | bytes 2359300
  96.9 0.9 copy-start.13
  148.9 71.2 %all-gather.3.cloned.1.call-start = ((), (), s32[]{:S(2)}) async-start(), calls=%async_computation.6 | async-start | bytes 1671168 | tf_op jit(solution)/shard_map/all_gather | solution.py:119
  178.2 5.7 %copy-start.4 = (f32[512,96]{0,1:T(8,128)}, f32[512,96]{0,1:T(8,128)S(1)}, u32[]{:S(2)}) copy-start(f32[512,96]{0,1:T(8,128)S(1)} %copy.59) | copy-start | bytes 589828
  179.4 8.9 %copy-start.6 = (f32[512,96]{0,1:T(8,128)}, f32[512,96]{0,1:T(8,128)S(1)}, u32[]{:S(2)}) copy-start(f32[512,96]{0,1:T(8,128)S(1)} %copy.60) | copy-start | bytes 589828
  180.2 69.9 %all-gather.5.cloned.1.call-start = ((), (), s32[]{:S(2)}) async-start(), calls=%async_computation.7 | async-start | bytes 2211840 | tf_op jit(solution)/shard_map/all_gather | solution.py:117
  180.4 8.0 %collective-permute-start.2 = (bf16[96,2]{1,0:T(8,128)(2,1)S(1)}, bf16[96,2]{1,0:T(8,128)(2,1)S(1)}, u32[]{:S(2)}, u32[]{:S(2)}) collective-permute-start(bf16[96,2]{1,0:T(8,128)(2,1)S(1)} %get-tuple-element.11), channel_id=1, source_target_pairs={{0,16},{1,17},{2,18},{3,19},{4,20},{5,21},{6,22},{7,23},{8,24},{9,... | collective-permute-start | bytes 1160 | tf_op jit(solution)/shard_map/ppermute | solution.py:15
  182.6 5.7 %collective-permute-start.3 = (bf16[96,2]{1,0:T(8,128)(2,1)S(1)}, bf16[96,2]{1,0:T(8,128)(2,1)S(1)}, u32[]{:S(2)}, u32[]{:S(2)}) collective-permute-start(bf16[96,2]{1,0:T(8,128)(2,1)S(1)} %get-tuple-element.10), channel_id=1, source_target_pairs={{16,0},{17,1},{18,2},{19,3},{20,4},{21,5},{22,6},{23,7},{24,8},{25... | collective-permute-start | bytes 1160 | tf_op jit(solution)/shard_map/ppermute | solution.py:17
  183.9 96.1 %reduce-scatter.5.cloned.1.call-start = ((), (), s32[]{:S(2)}) async-start(), calls=%async_computation.8 | async-start | bytes 2211840 | tf_op jit(solution)/shard_map/reduce_scatter | solution.py:139
  220.1 2.9 copy-start
  228.3 5.0 %copy-start.3 = (bf16[96,16,256]{2,0,1:T(8,128)(2,1)S(1)}, bf16[96,16,256]{2,0,1:T(8,128)(2,1)}, u32[]{:S(2)}) copy-start(bf16[96,16,256]{2,0,1:T(8,128)(2,1)} %copy-done.2) | copy-start | bytes 2359300
  228.3 5.0 %copy-start.14 = (f32[1536,256]{0,1:T(8,128)S(1)}, f32[1536,256]{0,1:T(8,128)}, u32[]{:S(2)}) copy-start(f32[1536,256]{0,1:T(8,128)} %fusion.14) | copy-start | bytes 4718596
  238.2 17.1 %collective-permute-start = (bf16[1536,2]{1,0:T(8,128)(2,1)}, bf16[1536,2]{1,0:T(8,128)(2,1)}, u32[]{:S(2)}, u32[]{:S(2)}) collective-permute-start(bf16[1536,2]{1,0:T(8,128)(2,1)} %get-tuple-element.6), channel_id=1, source_target_pairs={{16,0},{17,1},{18,2},{19,3},{20,4},{21,5},{22,6},{23,7},{24,8},{25... | collective-permute-start | bytes 18440 | tf_op jit(solution)/shard_map/ppermute | solution.py:17
  239.5 14.1 %collective-permute-start.1 = (bf16[1536,2]{1,0:T(8,128)(2,1)}, bf16[1536,2]{1,0:T(8,128)(2,1)}, u32[]{:S(2)}, u32[]{:S(2)}) collective-permute-start(bf16[1536,2]{1,0:T(8,128)(2,1)} %get-tuple-element.7), channel_id=1, source_target_pairs={{0,16},{1,17},{2,18},{3,19},{4,20},{5,21},{6,22},{7,23},{8,24},{9,... | collective-permute-start | bytes 18440 | tf_op jit(solution)/shard_map/ppermute | solution.py:15
  250.1 3.5 %copy-start.11 = (bf16[5,96,1536]{2,1,0:T(8,128)(2,1)S(1)}, bf16[5,96,1536]{2,1,0:T(8,128)(2,1)}, u32[]{:S(2)}) copy-start(bf16[5,96,1536]{2,1,0:T(8,128)(2,1)} %all-gather.5.cloned.1.call-done) | copy-start | bytes 4423684
  257.0 0.9 copy-start.5
  257.0 1.0 copy-start.7
  257.0 1.1 copy-start.10
Sparse Core Ops, SparseCore 0:
  149.0 26.4 reduce-scatter.2
  180.4 39.6 all-gather.2
  221.7 28.3 all-gather.4
  252.9 27.0 reduce-scatter.4
where the time goes:
time: 290 us; the launch traced here: 289 us
  waiting for transfers between devices  102 us (35%)
  blocking collectives  66.6 us (23%)
  matrix products  38.7 us (13%)
  local copies, waits for them, and re-layouts  34.8 us (12%)
  starting transfers between devices  23.1 us (8%)
  between operations  14.3 us (5%)
  other arithmetic  9.54 us (3%)
    all_to_all x1, blocking collectives, local(): lax.all_to_all(rows_back.reshape(model_width, 1, total_rows), 'exp', spli...  41.4 us
    all_gather x1, waiting for transfers between devices, local(): gathered = lax.all_gather(grad_pre_conv, 'exp', axis=0, tiled=True)  31.7 us
    reduce_scatter x1, waiting for transfers between devices, local(): lax.psum_scatter(moved_back, 'ctx', scatter_dimension=2, tiled=True)  26.2 us
    dot_general x8, matrix products, turned(): lax.dot_general(left.astype(jnp.float32), right.astype(jnp.float32), (dim...  21.9 us
    reduce_scatter x1, waiting for transfers between devices, local(): lax.psum_scatter(conv_grad.astype(jnp.bfloat16), 'ctx', scatter_dimension...  19.5 us
    all_to_all x1, waiting for transfers between devices, local(): lax.all_to_all(copied[1], 'exp', split_axis=1, concat_axis=0, tiled=True)  13.8 us
    all_gather x1, blocking collectives, local(): lax.all_gather(send_rows, 'ctx', axis=2, tiled=True)  13 us
    all_gather x1, blocking collectives, local(): lax.all_gather(send_grad, 'ctx', axis=2, tiled=True)  12.2 us
  transfers between devices with their start and end apart: 10, of which 7 were waited for; matrix products, arithmetic and copies ran while one was open for 15% of the time, Pallas kernels for 0%

commit v1 on v0

v1 whole, which is shorter than its diff:
```python
import jax
import jax.numpy as jnp
from jax import lax
from jax.sharding import PartitionSpec as P

BF16 = jnp.bfloat16
F32 = jnp.float32


def gelu_value(values):
    factor = 0.7978845608028654
    return 0.5 * values * (1.0 + jnp.tanh(factor * (values + 0.044715 * values * values * values)))


def gelu_slope(values):
    factor = 0.7978845608028654
    tangent = jnp.tanh(factor * (values + 0.044715 * values * values * values))
    return 0.5 * (1.0 + tangent) + 0.5 * values * (1.0 - tangent * tangent) * factor * (
        1.0 + 0.134145 * values * values
    )


def product(left, right, dims):
    return lax.dot_general(left, right, (dims, ((), ())), preferred_element_type=F32)


def swapped(block):
    return lax.ppermute(block, "ctx", [(0, 1), (1, 0)])


def local(inputs, pre_act, grad_out, conv_weight, expert_ids, gate_values, expert_in, expert_out):
    channels, bins = inputs.shape
    experts = lax.axis_size("exp")
    groups = lax.axis_size("ctx")
    capacity = 4 * bins // experts
    width = channels * experts
    kernel = conv_weight.shape[0]
    margin = kernel // 2
    pair = groups == 2
    me = lax.axis_index("ctx")

    ids = expert_ids.T
    names = jnp.arange(experts, dtype=jnp.int32)[:, None]
    chosen = [ids[k][None, :] == names for k in range(ids.shape[0])]
    named = sum(c.astype(BF16) for c in chosen)
    spot = jnp.arange(bins, dtype=jnp.int32)
    earlier = product(named, (spot[:, None] < spot[None, :]).astype(BF16), ((1,), (0,)))
    rows = jnp.arange(experts * capacity, dtype=jnp.int32)[:, None]
    picks = []
    for k, c in enumerate(chosen):
        slot = jnp.sum(jnp.where(c, earlier, 0.0), axis=0).astype(jnp.int32)
        picks.append((rows == (ids[k] * capacity + slot)[None, :]).astype(BF16))
    pick_any = sum(picks)
    pick_each = jnp.concatenate(picks, axis=1)

    pre_float = pre_act.astype(F32)
    grad_float = grad_out.astype(F32)
    activated = (inputs.astype(F32) + gelu_value(pre_float)).astype(BF16)
    gates = gate_values.T
    gated = jnp.concatenate(
        [(grad_float * gates[k][None, :]).astype(BF16) for k in range(len(picks))], axis=1
    )

    def to_experts(cells, pick):
        found = product(cells, pick, ((1,), (1,))).astype(BF16)
        found = found.reshape(channels, experts, capacity).transpose(1, 0, 2)
        found = lax.all_to_all(found, "exp", split_axis=0, concat_axis=0, tiled=True)
        found = found.reshape(width, capacity)
        if pair:
            return jnp.concatenate([found, swapped(found)], axis=1)
        return lax.all_gather(found, "ctx", axis=1, tiled=True)

    rows_in = to_experts(activated, pick_any)
    rows_grad = to_experts(gated, pick_each)

    first = expert_in[0]
    second = expert_out[0]
    hidden = product(first, rows_in, ((0,), (0,)))
    grad_hidden = product(second, rows_grad, ((1,), (0,)))
    grad_pre = (grad_hidden * gelu_slope(hidden)).astype(BF16)
    if pair:
        theirs = product(first, grad_pre[:, capacity:], ((1,), (0,))).astype(BF16)
        mine = product(first, grad_pre[:, :capacity], ((1,), (0,)))
        back = (mine + swapped(theirs).astype(F32)).astype(BF16)
    else:
        part = product(first, grad_pre, ((1,), (0,)))
        back = lax.psum_scatter(part, "ctx", scatter_dimension=1, tiled=True).astype(BF16)
    squashed = gelu_value(hidden).astype(BF16)
    grad_second = product(squashed, rows_grad, ((1,), (1,))).astype(BF16)
    grad_first = product(rows_in, grad_pre, ((1,), (1,))).astype(BF16)

    back = lax.all_to_all(
        back.reshape(experts, channels, capacity), "exp", split_axis=0, concat_axis=0, tiled=True
    )
    back = back.transpose(1, 0, 2).reshape(channels, experts * capacity)
    grad_total = grad_float + product(back, pick_any, ((1,), (0,)))
    grad_pre_conv = (grad_total * gelu_slope(pre_float)).astype(BF16)

    share = experts // groups
    moves = [
        (c * experts + e, (e // share) * experts + c * share + e % share)
        for c in range(groups)
        for e in range(experts)
    ]
    moved = lax.ppermute(grad_pre_conv, ("ctx", "exp"), moves)
    blocks = lax.all_gather(moved, "exp", axis=0, tiled=True).reshape(groups, -1, bins)

    if pair:
        other = swapped(inputs)
        low = jnp.where(me == 0, inputs, other)
        high = jnp.where(me == 0, other, inputs)
        all_inputs = jnp.concatenate([low, high], axis=1)
    else:
        all_inputs = lax.all_gather(inputs, "ctx", axis=1, tiled=True)
    total = groups * bins
    padded = jnp.pad(all_inputs, ((0, 0), (margin, margin)))
    shifted = jnp.concatenate([padded[:, k : k + total] for k in range(kernel)], axis=0)
    weight = conv_weight.reshape(kernel * channels, -1)
    spread = jnp.concatenate(
        [product(weight, blocks[c], ((1,), (0,))) for c in range(groups)], axis=1
    )
    spread = jnp.pad(spread.reshape(kernel, channels, total), ((0, 0), (0, 0), (margin, margin)))
    conv_back = sum(
        spread[k, :, 2 * margin - k : 2 * margin - k + total] for k in range(kernel)
    )
    if pair:
        low, high = conv_back[:, :bins], conv_back[:, bins:]
        mine = jnp.where(me == 0, low, high)
        theirs = jnp.where(me == 0, high, low).astype(BF16)
        conv_back = mine + swapped(theirs).astype(F32)
    else:
        conv_back = lax.psum_scatter(conv_back, "ctx", scatter_dimension=1, tiled=True)
    grad_inputs = (grad_total + conv_back).astype(BF16)
    grad_conv = sum(
        product(shifted[:, c * bins : (c + 1) * bins], blocks[c], ((1,), (1,)))
        for c in range(groups)
    )
    return (
        grad_inputs,
        grad_conv.reshape(kernel, channels, -1),
        grad_first[None],
        grad_second[None],
    )


def solution(mesh):
    placed = (
        P("exp", "ctx"),
        P("exp", "ctx"),
        P("exp", "ctx"),
        P(None, "exp", "ctx"),
        P("ctx", None),
        P("ctx", None),
        P("exp", None, "ctx"),
        P("exp", "ctx", None),
    )
    return jax.shard_map(
        local,
        mesh=mesh,
        in_specs=placed,
        out_specs=(
            P("exp", "ctx"),
            P(None, "exp", "ctx"),
            P("exp", None, "ctx"),
            P("exp", "ctx", None),
        ),
        check_vma=False,
    )
```

time: 290 us -> 157 us (0.54)
  blocking collectives: 66.6 us -> 15.9 us
  waiting for transfers between devices: 102 us -> 61 us
  local copies, waits for them, and re-layouts: 34.8 us -> 3.83 us
  matrix products: 38.7 us -> 28.2 us
  starting transfers between devices: 23.1 us -> 29.5 us
  other arithmetic: 9.54 us -> 3.93 us
    reduce_scatter x2 -> x0, waiting for transfers between devices: 45.7 us -> none  [the longest x1 26.2 us: local(): lax.psum_scatter(moved_back, 'ctx', scatter_dimension=2, tiled=True)]
    all_to_all x1, blocking collectives: 41.4 us -> 15.9 us  [local(): lax.all_to_all(back.reshape(experts, channels, capacity), 'exp', split_ax...]
    all_gather x2 -> x0, blocking collectives: 25.2 us -> none  [the longest x1 13 us: local(): lax.all_gather(send_rows, 'ctx', axis=2, tiled=True)]
    gather x7 -> x0, local copies, waits for them, and re-layouts: 14.3 us -> none  [the longest x1 6.18 us: local(): send_rows = act_pad[:, row_table].reshape(channels, experts, capacity)]
    all_gather x2 -> x1, waiting for transfers between devices: 36.2 us -> 24 us  [local(): lax.all_gather(moved, 'exp', axis=0, tiled=True).reshape(groups, -1, bins)]
    ppermute x4 -> x6, waiting for transfers between devices: 6.16 us -> 18.2 us  [the longest x5 18.2 us: swapped(): return lax.ppermute(block, 'ctx', [(0, 1), (1, 0)])]
    dot_general x15 -> x14, matrix products: 38.7 us -> 28.2 us  [product(): lax.dot_general(left, right, (dims, ((), ())), preferred_element_type=F32)]
    scatter x2 -> x0, local copies, waits for them, and re-layouts: 8.63 us -> none  [the longest x1 4.32 us: local(): jnp.full((experts * capacity,), bins_local, jnp.int32).at[targets]]
  transfers between devices with their start and end apart: 10 -> 9, of which waited for: 7 -> 7; matrix products, arithmetic and copies ran while one was open for 15% -> 12% of each run, Pallas kernels for 0% -> 0%
where the time goes in v1:
time: 157 us
  waiting for transfers between devices  61 us (39%)
  starting transfers between devices  29.5 us (19%)
  matrix products  28.2 us (18%)
  blocking collectives  15.9 us (10%)
  between operations  14.4 us (9%)
  other arithmetic  3.93 us (3%)
  local copies, waits for them, and re-layouts  3.83 us (2%)
    dot_general x14, matrix products, product(): lax.dot_general(left, right, (dims, ((), ())), preferred_element_type=F32)  28.2 us
    all_gather x1, waiting for transfers between devices, local(): lax.all_gather(moved, 'exp', axis=0, tiled=True).reshape(groups, -1, bins)  24 us
    all_to_all x2, waiting for transfers between devices, to_experts(): lax.all_to_all(found, 'exp', split_axis=0, concat_axis=0, tiled=True)  18.7 us
    ppermute x5, waiting for transfers between devices, swapped(): return lax.ppermute(block, 'ctx', [(0, 1), (1, 0)])  18.2 us
    ppermute x5, starting transfers between devices, swapped(): return lax.ppermute(block, 'ctx', [(0, 1), (1, 0)])  17.6 us
    all_to_all x1, blocking collectives, local(): lax.all_to_all(back.reshape(experts, channels, capacity), 'exp', split_ax...  15.9 us
    all_to_all x2, starting transfers between devices, to_experts(): lax.all_to_all(found, 'exp', split_axis=0, concat_axis=0, tiled=True)  11 us
  transfers between devices with their start and end apart: 9, of which 7 were waited for; matrix products, arithmetic and copies ran while one was open for 12% of the time, Pallas kernels for 0%

profile of v1, /device:TPU:0, one launch (start us, length us, event | category | flops | bytes accessed | tf_op | source)
XLA Modules:
  0.0 156.7 jit_solution(602203953908310480)
XLA Ops:
  7.2 0.0 copy-start
  7.2 0.8 fusion.125
  8.0 0.2 select_reduce_fusion.1
  8.2 0.8 multiply_add_fusion.2
  9.0 2.1 %fusion.45 = bf16[12,16,8,128]{3,2,1,0:T(8,128)(2,1)S(1)} fusion(s32[512]{0:T(512)S(1)} %bitcast.127, s32[512]{0:T(512)S(1)} %bitcast.124, bf16[96,512]{1,0:T(8,128)(2,1)} %param.9, bf16[96,512]{1,0:T(8,128)(2,1)} %param.8), kind=kOutput, calls=%fused_computation.47 | convolution fusion | flops 210501632 | bytes 593920 | tf_op jit(solution)/shard_map/dot_general | solution.py:24
  11.1 0.0 copy-start.5
  11.1 0.0 copy-start.3
  11.1 0.8 copy.27
  11.9 7.4 %all-to-all-start.1 = ((bf16[16,96,128]{2,1,0:T(8,128)(2,1)}), bf16[16,96,128]{2,1,0:T(8,128)(2,1)S(1)}, u32[]{:S(2)}, u32[]{:S(2)}) async-start(bf16[16,96,128]{2,1,0:T(8,128)(2,1)} %bitcast.106), calls=%async_computation.1 | async-start | bytes 786432 | tf_op jit(solution)/shard_map/all_to_all | solution.py:67
  19.3 0.0 copy-done.5
  19.3 0.0 copy-done.3
  19.4 1.7 %fusion.14 = (bf16[2048,512]{1,0:T(8,128)(2,1)S(1)}, bf16[2048,512]{1,0:T(8,128)(2,1)S(1)}) fusion(s32[512]{0:T(512)S(1)} %bitcast.125, s32[512]{0:T(512)S(1)} %bitcast.128), kind=kLoop, calls=%fused_computation.18 | loop fusion | flops 4194304 | bytes 4198400 | tf_op jit(solution)/shard_map/convert_element_type | solution.py:52
  21.1 1.4 fusion.46
  22.5 0.8 copy.28
  23.3 8.2 %all-to-all-done.1 = bf16[16,96,128]{2,1,0:T(8,128)(2,1)S(1)} async-done(((bf16[16,96,128]{2,1,0:T(8,128)(2,1)}), bf16[16,96,128]{2,1,0:T(8,128)(2,1)S(1)}, u32[]{:S(2)}, u32[]{:S(2)}) %all-to-all-start.1) | async-done | bytes 393248 | tf_op jit(solution)/shard_map/all_to_all | solution.py:67
  31.5 3.7 %all-to-all-start = ((bf16[16,96,128]{2,1,0:T(8,128)(2,1)}), bf16[16,96,128]{2,1,0:T(8,128)(2,1)S(1)}, u32[]{:S(2)}, u32[]{:S(2)}) async-start(bf16[16,96,128]{2,1,0:T(8,128)(2,1)} %bitcast.108), calls=%async_computation | async-start | bytes 786432 | tf_op jit(solution)/shard_map/all_to_all | solution.py:67
  35.2 0.0 all-gather.2.cloned.1.call-start
  35.3 1.6 %collective-permute-start.1 = (bf16[1536,128]{1,0:T(8,128)(2,1)S(1)}, bf16[1536,128]{1,0:T(8,128)(2,1)S(1)}, u32[]{:S(2)}, u32[]{:S(2)}) collective-permute-start(bf16[1536,128]{1,0:T(8,128)(2,1)S(1)} %bitcast.116), channel_id=1, source_target_pairs={{0,16},{16,0},{1,17},{17,1},{2,18},{18,2},{3,19},{19,3},{4,20},{20... | collective-permute-start | bytes 1179656 | tf_op jit(solution)/shard_map/ppermute | solution.py:28
  36.9 10.5 %all-to-all-done = bf16[16,96,128]{2,1,0:T(8,128)(2,1)S(1)} async-done(((bf16[16,96,128]{2,1,0:T(8,128)(2,1)}), bf16[16,96,128]{2,1,0:T(8,128)(2,1)S(1)}, u32[]{:S(2)}, u32[]{:S(2)}) %all-to-all-start) | async-done | bytes 393248 | tf_op jit(solution)/shard_map/all_to_all | solution.py:67
  47.4 1.5 collective-permute-start
  48.9 0.0 collective-permute-done.1
  48.9 3.9 %fusion.22 = f32[1536,256]{0,1:T(8,128)S(1)} fusion(bf16[1,1536,1536]{2,1,0:T(8,128)(2,1)} %param.14, bf16[1536,128]{1,0:T(8,128)(2,1)S(1)} %collective-permute-done.1, bf16[1536,128]{1,0:T(8,128)(2,1)S(1)} %bitcast.117), kind=kOutput, calls=%fused_computation.22 | convolution fusion | flops 1209532416 | bytes 7077888 | tf_op jit(solution)/shard_map/dot_general | solution.py:24
  52.8 0.0 copy-done.6
  52.8 0.0 copy-start.9
  52.9 0.0 slice-start.1
  52.9 5.6 %collective-permute-done = bf16[1536,128]{1,0:T(8,128)(2,1)S(1)} collective-permute-done((bf16[1536,128]{1,0:T(8,128)(2,1)S(1)}, bf16[1536,128]{1,0:T(8,128)(2,1)S(1)}, u32[]{:S(2)}, u32[]{:S(2)}) %collective-permute-start) | collective-permute-done | bytes 393248 | tf_op jit(solution)/shard_map/ppermute | solution.py:28
  58.5 0.0 slice-done.2
  58.5 0.0 slice-done.3
  58.5 2.1 %fusion.25 = bf16[1536,256]{0,1:T(8,128)(2,1)S(1)} fusion(bf16[1,1536,1536]{2,1,0:T(8,128)(2,1)S(1)} %bitcast.138, f32[1536,256]{0,1:T(8,128)S(1)} %fusion.22, bf16[1536,128]{1,0:T(8,128)(2,1)S(1)} %collective-permute-done, bf16[1536,128]{1,0:T(8,128)(2,1)S(1)} %bitcast.120), kind=kOutput, calls=%fused_computation.23 | convolution fusion | flops 1217003520 | bytes 7864320 | tf_op jit(solution)/shard_map/dot_general | solution.py:24
  60.6 0.0 copy-done.9
  60.6 1.6 %fusion.37 = bf16[1536,128]{0,1:T(8,128)(2,1)S(1)} fusion(bf16[1,1536,1536]{2,1,0:T(8,128)(2,1)S(1)} %bitcast.112, bf16[1536,256]{0,1:T(8,128)(2,1)S(1)} %fusion.25), kind=kOutput, calls=%fused_computation.30 | convolution fusion | flops 604176384 | bytes 5505024 | tf_op jit(solution)/shard_map/dot_general | solution.py:24
  62.3 1.6 %collective-permute-start.2 = (bf16[1536,128]{0,1:T(8,128)(2,1)S(1)}, bf16[1536,128]{0,1:T(8,128)(2,1)S(1)}, u32[]{:S(2)}, u32[]{:S(2)}) collective-permute-start(bf16[1536,128]{0,1:T(8,128)(2,1)S(1)} %fusion.37), channel_id=1, source_target_pairs={{0,16},{16,0},{1,17},{17,1},{2,18},{18,2},{3,19},{19,3},{4,20},{20... | collective-permute-start | bytes 1179656 | tf_op jit(solution)/shard_map/ppermute | solution.py:28
  63.9 8.8 %collective-permute-done.2 = bf16[1536,128]{0,1:T(8,128)(2,1)S(1)} collective-permute-done((bf16[1536,128]{0,1:T(8,128)(2,1)S(1)}, bf16[1536,128]{0,1:T(8,128)(2,1)S(1)}, u32[]{:S(2)}, u32[]{:S(2)}) %collective-permute-start.2) | collective-permute-done | bytes 393248 | tf_op jit(solution)/shard_map/ppermute | solution.py:28
  72.6 1.7 %add_convert_fusion = bf16[1536,128]{0,1:T(8,128)(2,1)S(1)} fusion(bf16[1536,128]{0,1:T(8,128)(2,1)S(1)} %collective-permute-done.2, bf16[1,1536,1536]{2,1,0:T(8,128)(2,1)S(1)} %bitcast.112, bf16[1536,256]{0,1:T(8,128)(2,1)S(1)} %fusion.25), kind=kOutput, calls=%fused_computation.54 | convolution fusion | flops 604569600 | bytes 5898240 | tf_op jit(solution)/shard_map/dot_general | solution.py:24
  74.3 0.2 copy.14
  74.5 15.9 %all_to_all.15 = bf16[16,96,128]{2,1,0:T(8,128)(2,1)S(1)} all-to-all(bf16[16,96,128]{2,1,0:T(8,128)(2,1)S(1)} %bitcast.114), channel_id=1, replica_groups=mesh['ctx'=2,'exp'=16] {'exp'}, dimensions={0} | all-to-all | bytes 786432 | tf_op jit(solution)/shard_map/all_to_all | solution.py:92
  90.5 2.0 %fusion.90 = (bf16[96,512]{1,0:T(8,128)(2,1)S(1)}, f32[96,512]{1,0:T(8,128)S(1)}) fusion(bf16[96,512]{1,0:T(8,128)(2,1)} %param.9, s32[512]{0:T(512)S(1)} %bitcast.129, s32[512]{0:T(512)S(1)} %bitcast.126, bf16[96,512]{1,0:T(8,128)(2,1)S(1)} %copy-done.3, bf16[16,96,128]{2,1,0:T(8,128)(2,1)S(1)} %all_to_all.15), kind=kOutput, calls=%fused_computation.98 | convolution fusion | flops 210796544 | bytes 888832 | tf_op jit(solution)/shard_map/dot_general | solution.py:24
  92.4 0.8 collective-permute-start.3
  93.3 0.0 collective-permute-done.3
  93.3 0.0 copy-start.2
  93.3 0.6 copy-done.2
  93.9 0.0 all-gather.2.cloned.1.call-update
  94.0 0.0 copy-done.4
  94.0 11.3 %collective-permute-start.5 = (bf16[96,512]{1,0:T(8,128)(2,1)S(1)}, bf16[96,512]{1,0:T(8,128)(2,1)S(1)}, u32[]{:S(2)}, u32[]{:S(2)}) collective-permute-start(bf16[96,512]{1,0:T(8,128)(2,1)S(1)} %copy-done.4), channel_id=1, source_target_pairs={{0,16},{16,0},{1,17},{17,1},{2,18},{18,2},{3,19},{19,3},{4,20},{20... | collective-permute-start | bytes 294920 | tf_op jit(solution)/shard_map/ppermute | solution.py:28
  105.3 2.6 %collective-permute-done.5 = bf16[96,512]{1,0:T(8,128)(2,1)S(1)} collective-permute-done((bf16[96,512]{1,0:T(8,128)(2,1)S(1)}, bf16[96,512]{1,0:T(8,128)(2,1)S(1)}, u32[]{:S(2)}, u32[]{:S(2)}) %collective-permute-start.5) | collective-permute-done | bytes 98336 | tf_op jit(solution)/shard_map/ppermute | solution.py:28
  107.9 0.1 slice_dynamic-update-slice_fusion.3
  108.1 0.1 slice_dynamic-update-slice_fusion.2
  108.2 0.1 slice_dynamic-update-slice_fusion.1
  108.4 0.1 slice_dynamic-update-slice_fusion
  108.5 0.0 copy-start.10
  108.5 4.7 %fusion = bf16[1,1536,1536]{2,1,0:T(8,128)(2,1)} fusion(bf16[1536,256]{0,1:T(8,128)(2,1)S(1)} %fusion.25, bf16[1536,128]{1,0:T(8,128)(2,1)} %copy-done.6, bf16[1536,128]{1,0:T(8,128)(2,1)S(1)} %bitcast.118), kind=kOutput, calls=%fused_computation.2 | convolution fusion | flops 1211891712 | bytes 6291456 | tf_op jit(solution)/shard_map/dot_general | solution.py:24
  113.2 0.0 copy-done.8
  113.2 3.8 %fusion.1 = bf16[1,1536,1536]{2,1,0:T(8,128)(2,1)} fusion(f32[1536,256]{0,1:T(8,128)S(1)} %copy-done.10, bf16[1536,128]{1,0:T(8,128)(2,1)S(1)} %copy-done.8, bf16[1536,128]{1,0:T(8,128)(2,1)S(1)} %bitcast.121), kind=kOutput, calls=%fused_computation.3 | convolution fusion | flops 1215430656 | bytes 7077888 | tf_op jit(solution)/shard_map/dot_general | solution.py:24
  117.1 24.0 %all-gather.2.cloned.1.call-done = bf16[1536,512]{1,0:T(8,128)(2,1)} async-done(((bf16[96,512]{1,0:T(8,128)(2,1)}), bf16[1536,512]{1,0:T(8,128)(2,1)}) %all-gather.2.cloned.1.call-update) | async-done | bytes 1572880 | tf_op jit(solution)/shard_map/all_gather | solution.py:106
  141.1 1.8 %convolution_bitcast_fusion = f32[480,512]{1,0:T(8,128)S(1)} fusion(bf16[480,768]{1,0:T(8,128)(2,1)S(1)} %bitcast.109, bf16[1536,512]{1,0:T(8,128)(2,1)} %all-gather.2.cloned.1.call-done), kind=kOutput, calls=%fused_computation.45 | convolution fusion | flops 377487360 | bytes 2506752 | tf_op jit(solution)/shard_map/dot_general | solution.py:24
  142.9 0.0 copy-done.1
  142.9 0.5 convolution_bitcast_fusion.1
  143.5 0.2 pad_maximum_fusion
  143.6 0.5 fusion.70
  144.1 1.5 collective-permute-start.4
  145.7 0.6 fusion.54
  146.3 1.7 %convolution_add_fusion = f32[480,768]{1,0:T(8,128)} fusion(f32[480,768]{1,0:T(8,128)S(1)} %fusion.54, bf16[1536,512]{1,0:T(8,128)(2,1)S(1)} %copy-done.1, bf16[480,1024]{1,0:T(8,128)(2,1)S(1)} %slice_dynamic-update-slice_fusion), kind=kOutput, calls=%fused_computation.44 | convolution fusion | flops 377856000 | bytes 4227072 | tf_op jit(solution)/shard_map/dot_general | solution.py:24
  148.0 1.2 collective-permute-done.4
  149.2 0.7 add_convert_fusion.1
  (23 shorter events, 0.1 us)
Async XLA Ops:
  7.2 133.9 %copy-start = (bf16[5,96,768]{2,1,0:T(8,128)(2,1)S(1)}, bf16[5,96,768]{2,1,0:T(8,128)(2,1)}, u32[]{:S(2)}) copy-start(bf16[5,96,768]{2,1,0:T(8,128)(2,1)} %param.11) | copy-start | bytes 2211844
  11.1 8.2 %copy-start.5 = (f32[512,2]{0,1:T(2,128)S(1)}, f32[512,2]{0,1:T(2,128)}, u32[]{:S(2)}) copy-start(f32[512,2]{0,1:T(2,128)} %param.13) | copy-start | bytes 12292
  11.1 8.2 %copy-start.3 = (bf16[96,512]{1,0:T(8,128)(2,1)S(1)}, bf16[96,512]{1,0:T(8,128)(2,1)}, u32[]{:S(2)}) copy-start(bf16[96,512]{1,0:T(8,128)(2,1)} %param.10) | copy-start | bytes 294916
  11.9 19.6 %all-to-all-start.1 = ((bf16[16,96,128]{2,1,0:T(8,128)(2,1)}), bf16[16,96,128]{2,1,0:T(8,128)(2,1)S(1)}, u32[]{:S(2)}, u32[]{:S(2)}) async-start(bf16[16,96,128]{2,1,0:T(8,128)(2,1)} %bitcast.106), calls=%async_computation.1 | async-start | bytes 786432 | tf_op jit(solution)/shard_map/all_to_all | solution.py:67
  31.5 27.0 %slice-start.2 = ((s8[4718592]{0:T(1024)(128)(4,1)}), s8[524288]{0:T(1024)(128)(4,1)S(1)}, s32[]{:S(2)}) async-start(s8[4718592]{0:T(1024)(128)(4,1)} %bitcast.137), calls=%async_computation.6 | async-start | bytes 1048576
  31.5 15.9 %all-to-all-start = ((bf16[16,96,128]{2,1,0:T(8,128)(2,1)}), bf16[16,96,128]{2,1,0:T(8,128)(2,1)S(1)}, u32[]{:S(2)}, u32[]{:S(2)}) async-start(bf16[16,96,128]{2,1,0:T(8,128)(2,1)} %bitcast.108), calls=%async_computation | async-start | bytes 786432 | tf_op jit(solution)/shard_map/all_to_all | solution.py:67
  35.2 105.9 %all-gather.2.cloned.1.call-start = ((), (), s32[]{:S(2)}) async-start(), calls=%async_computation.3 | async-start | bytes 1671168 | tf_op jit(solution)/shard_map/all_gather | solution.py:106
  35.3 13.6 %collective-permute-start.1 = (bf16[1536,128]{1,0:T(8,128)(2,1)S(1)}, bf16[1536,128]{1,0:T(8,128)(2,1)S(1)}, u32[]{:S(2)}, u32[]{:S(2)}) collective-permute-start(bf16[1536,128]{1,0:T(8,128)(2,1)S(1)} %bitcast.116), channel_id=1, source_target_pairs={{0,16},{16,0},{1,17},{17,1},{2,18},{18,2},{3,19},{19,3},{4,20},{20... | collective-permute-start | bytes 1179656 | tf_op jit(solution)/shard_map/ppermute | solution.py:28
  47.4 11.1 %slice-start.3 = ((s8[4718592]{0:T(1024)(128)(4,1)}), s8[4194304]{0:T(1024)(128)(4,1)S(1)}, s32[]{:S(2)}) async-start(s8[4718592]{0:T(1024)(128)(4,1)} %bitcast.137), calls=%async_computation.7 | async-start | bytes 8388608
  47.4 11.1 %collective-permute-start = (bf16[1536,128]{1,0:T(8,128)(2,1)S(1)}, bf16[1536,128]{1,0:T(8,128)(2,1)S(1)}, u32[]{:S(2)}, u32[]{:S(2)}) collective-permute-start(bf16[1536,128]{1,0:T(8,128)(2,1)S(1)} %bitcast.119), channel_id=1, source_target_pairs={{0,16},{16,0},{1,17},{17,1},{2,18},{18,2},{3,19},{19,3},{4,20},{20... | collective-permute-start | bytes 1179656 | tf_op jit(solution)/shard_map/ppermute | solution.py:28
  48.9 3.9 %copy-start.6 = (bf16[1536,128]{1,0:T(8,128)(2,1)}, bf16[1536,128]{1,0:T(8,128)(2,1)S(1)}, u32[]{:S(2)}) copy-start(bf16[1536,128]{1,0:T(8,128)(2,1)S(1)} %collective-permute-done.1) | copy-start | bytes 1179652
  48.9 11.7 %slice-start = ((s8[4718592]{0:T(1024)(128)(4,1)}), s8[4194304]{0:T(1024)(128)(4,1)S(1)}, s32[]{:S(2)}) async-start(s8[4718592]{0:T(1024)(128)(4,1)} %bitcast.111), calls=%async_computation.4 | async-start | bytes 8388608
  52.8 7.7 %copy-start.9 = (f32[1536,256]{0,1:T(8,128)}, f32[1536,256]{0,1:T(8,128)S(1)}, u32[]{:S(2)}) copy-start(f32[1536,256]{0,1:T(8,128)S(1)} %fusion.22) | copy-start | bytes 4718596
  52.9 7.8 %slice-start.1 = ((s8[4718592]{0:T(1024)(128)(4,1)}), s8[524288]{0:T(1024)(128)(4,1)S(1)}, s32[]{:S(2)}) async-start(s8[4718592]{0:T(1024)(128)(4,1)} %bitcast.111), calls=%async_computation.5 | async-start | bytes 1048576
  58.5 2.1 %copy-start.7 = (bf16[1536,128]{1,0:T(8,128)(2,1)}, bf16[1536,128]{1,0:T(8,128)(2,1)S(1)}, u32[]{:S(2)}) copy-start(bf16[1536,128]{1,0:T(8,128)(2,1)S(1)} %collective-permute-done) | copy-start | bytes 1179652
  62.3 10.3 %collective-permute-start.2 = (bf16[1536,128]{0,1:T(8,128)(2,1)S(1)}, bf16[1536,128]{0,1:T(8,128)(2,1)S(1)}, u32[]{:S(2)}, u32[]{:S(2)}) collective-permute-start(bf16[1536,128]{0,1:T(8,128)(2,1)S(1)} %fusion.37), channel_id=1, source_target_pairs={{0,16},{16,0},{1,17},{17,1},{2,18},{18,2},{3,19},{19,3},{4,20},{20... | collective-permute-start | bytes 1179656 | tf_op jit(solution)/shard_map/ppermute | solution.py:28
  90.4 3.5 %copy-start.4 = (bf16[96,512]{1,0:T(8,128)(2,1)S(1)}, bf16[96,512]{1,0:T(8,128)(2,1)}, u32[]{:S(2)}) copy-start(bf16[96,512]{1,0:T(8,128)(2,1)} %param.8) | copy-start | bytes 294916
  92.4 0.9 collective-permute-start.3
  93.3 0.6 copy-start.2
  94.0 13.9 %collective-permute-start.5 = (bf16[96,512]{1,0:T(8,128)(2,1)S(1)}, bf16[96,512]{1,0:T(8,128)(2,1)S(1)}, u32[]{:S(2)}, u32[]{:S(2)}) collective-permute-start(bf16[96,512]{1,0:T(8,128)(2,1)S(1)} %copy-done.4), channel_id=1, source_target_pairs={{0,16},{16,0},{1,17},{17,1},{2,18},{18,2},{3,19},{19,3},{4,20},{20... | collective-permute-start | bytes 294920 | tf_op jit(solution)/shard_map/ppermute | solution.py:28
  108.5 4.7 %copy-start.8 = (bf16[1536,128]{1,0:T(8,128)(2,1)S(1)}, bf16[1536,128]{1,0:T(8,128)(2,1)}, u32[]{:S(2)}) copy-start(bf16[1536,128]{1,0:T(8,128)(2,1)} %copy-done.7) | copy-start | bytes 1179652
  108.5 4.7 %copy-start.10 = (f32[1536,256]{0,1:T(8,128)S(1)}, f32[1536,256]{0,1:T(8,128)}, u32[]{:S(2)}) copy-start(f32[1536,256]{0,1:T(8,128)} %copy-done.9) | copy-start | bytes 4718596
  141.1 1.8 %copy-start.1 = (bf16[1536,512]{1,0:T(8,128)(2,1)S(1)}, bf16[1536,512]{1,0:T(8,128)(2,1)}, u32[]{:S(2)}) copy-start(bf16[1536,512]{1,0:T(8,128)(2,1)} %all-gather.2.cloned.1.call-done) | copy-start | bytes 4718596
  144.1 5.0 %collective-permute-start.4 = (bf16[96,512]{1,0:T(8,128)(2,1)S(1)}, bf16[96,512]{1,0:T(8,128)(2,1)S(1)}, u32[]{:S(2)}, u32[]{:S(2)}) collective-permute-start(bf16[96,512]{1,0:T(8,128)(2,1)S(1)} %select_convert_fusion), channel_id=1, source_target_pairs={{0,16},{16,0},{1,17},{17,1},{2,18},{18,2},{3,19},{19,3},{4,20},{20... | collective-permute-start | bytes 294920 | tf_op jit(solution)/shard_map/ppermute | solution.py:28
Sparse Core Ops, SparseCore 0:
  94.1 46.9 all-gather.1

commit v2 on v1

--- a/solution.py
+++ b/solution.py
@@ -1,6 +1,8 @@
 import jax
 import jax.numpy as jnp
 from jax import lax
+from jax.experimental import pallas as pl
+from jax.experimental.pallas import tpu as pltpu
 from jax.sharding import PartitionSpec as P
 
 BF16 = jnp.bfloat16
@@ -26,6 +28,113 @@
 
 def swapped(block):
     return lax.ppermute(block, "ctx", [(0, 1), (1, 0)])
+
+
+def greet(barrier, peers):
+    for peer in peers:
+        pl.semaphore_signal(barrier, inc=1, device_id=peer, device_id_type=pl.DeviceIdType.MESH)
+
+
+def remote(source, target, sent, received, device):
+    return pltpu.make_async_remote_copy(
+        src_ref=source,
+        dst_ref=target,
+        send_sem=sent,
+        recv_sem=received,
+        device_id=device,
+        device_id_type=pl.DeviceIdType.MESH,
+    )
+
+
+def gather_kernel(cells, out, move_sem, z_sent, z_got, x_sent, x_got, c_sent, c_got):
+    c, e = lax.axis_index("ctx"), lax.axis_index("exp")
+    size = out.shape[0]
+    share = size // 2
+    high, low = lax.div(e, share), lax.rem(e, share)
+    there = (high, c * share + low)
+    across = e + 2 - 4 * lax.rem(lax.div(e, 2), 2)
+    twin = e + 1 - 2 * lax.rem(e, 2)
+    steps = size // 4
+    ring = [lax.rem(e + 4 * d, size) for d in range(1, steps)]
+    barrier = pltpu.get_barrier_semaphore()
+
+    @pl.when(high != c)
+    def _():
+        greet(barrier, [there])
+
+    greet(barrier, [(c, r) for r in ring] + [(c, across), (c, twin)])
+    pl.semaphore_wait(barrier, steps + 1 + (high != c).astype(jnp.int32))
+
+    @pl.when(high != c)
+    def _():
+        remote(cells, out.at[there[1]], move_sem.at[0], move_sem.at[1], there).start()
+        remote(cells, out.at[there[1]], move_sem.at[0], move_sem.at[1], there).wait_send()
+        remote(cells, out.at[e], move_sem.at[0], move_sem.at[1], there).wait_recv()
+
+    @pl.when(high == c)
+    def _():
+        copy = pltpu.make_async_copy(cells, out.at[e], move_sem.at[0])
+        copy.start()
+        copy.wait()
+
+    def back(base, d):
+        return lax.rem(base + size - 4 * d, size)
+
+    def along_z(slot, d):
+        return remote(
+            out.at[slot], out.at[slot], z_sent.at[d - 1], z_got.at[d - 1], (c, ring[d - 1])
+        )
+
+    def along_x(slot, j):
+        return remote(out.at[slot], out.at[slot], x_sent.at[j], x_got.at[j], (c, across))
+
+    def to_twin(slot, j):
+        return remote(out.at[slot], out.at[slot], c_sent.at[j], c_got.at[j], (c, twin))
+
+    for d in range(1, steps):
+        along_z(e, d).start()
+    along_x(e, 0).start()
+    to_twin(e, 0).start()
+    for d in range(steps):
+        if d:
+            along_z(back(e, d), d).wait_recv()
+            along_x(back(e, d), d).start()
+            to_twin(back(e, d), d).start()
+        along_x(back(across, d), d).wait_recv()
+        to_twin(back(across, d), steps + d).start()
+    twin_across = twin + across - e
+    for d in range(steps):
+        to_twin(back(twin, d), d).wait_recv()
+        to_twin(back(twin_across, d), steps + d).wait_recv()
+    for d in range(1, steps):
+        along_z(e, d).wait_send()
+    for d in range(steps):
+        along_x(back(e, d), d).wait_send()
+        to_twin(back(e, d), d).wait_send()
+        to_twin(back(across, d), steps + d).wait_send()
+
+
+def gathered(cells, size):
+    steps = size // 4
+    dma = pltpu.SemaphoreType.DMA
+    return pl.pallas_call(
+        gather_kernel,
+        out_shape=jax.ShapeDtypeStruct((size,) + cells.shape, cells.dtype),
+        in_specs=[pl.BlockSpec(memory_space=pltpu.VMEM)],
+        out_specs=pl.BlockSpec(memory_space=pltpu.VMEM),
+        scratch_shapes=[
+            dma((2,)),
+            dma((steps - 1,)),
+            dma((steps - 1,)),
+            dma((steps,)),
+            dma((steps,)),
+            dma((2 * steps,)),
+            dma((2 * steps,)),
+        ],
+        compiler_params=pltpu.CompilerParams(
+            collective_id=0, has_side_effects=True, vmem_limit_bytes=24 * 2**20
+        ),
+    )(cells)
 
 
 def local(inputs, pre_act, grad_out, conv_weight, expert_ids, gate_values, expert_in, expert_out):
@@ -97,13 +206,16 @@
     grad_pre_conv = (grad_total * gelu_slope(pre_float)).astype(BF16)
 
     share = experts // groups
-    moves = [
-        (c * experts + e, (e // share) * experts + c * share + e % share)
-        for c in range(groups)
-        for e in range(experts)
-    ]
-    moved = lax.ppermute(grad_pre_conv, ("ctx", "exp"), moves)
-    blocks = lax.all_gather(moved, "exp", axis=0, tiled=True).reshape(groups, -1, bins)
+    if pair and experts == 16:
+        blocks = gathered(grad_pre_conv, experts).reshape(groups, -1, bins)
+    else:
+        moves = [
+            (c * experts + e, (e // share) * experts + c * share + e % share)
+            for c in range(groups)
+            for e in range(experts)
+        ]
+        moved = lax.ppermute(grad_pre_conv, ("ctx", "exp"), moves)
+        blocks = lax.all_gather(moved, "exp", axis=0, tiled=True).reshape(groups, -1, bins)
 
     if pair:
         other = swapped(inputs)

time: 157 us -> 126 us (0.80)
  Pallas kernels: 0 us -> 26.8 us
  waiting for transfers between devices: 61 us -> 39 us
  blocking collectives: 15.9 us -> 0 us
  between operations: 14.4 us -> 1.01 us
  starting transfers between devices: 29.5 us -> 21.7 us
    pallas_call x0 -> x1, Pallas kernels: none -> 26.8 us  [gathered(): pl.pallas_call(gather_kernel, out_shape=jax.ShapeDtypeStruct((size,) + ce...]
    all_gather x1 -> x0, waiting for transfers between devices: 24 us -> none  [local(): lax.all_gather(moved, 'exp', axis=0, tiled=True).reshape(groups, -1, bins)]
    all_to_all x1 -> x0, blocking collectives: 15.9 us -> none  [local(): lax.all_to_all(back.reshape(experts, channels, capacity), 'exp', split_ax...]
    ppermute x5, starting transfers between devices: 17.6 us -> 5.42 us  [swapped(): return lax.ppermute(block, 'ctx', [(0, 1), (1, 0)])]
    all_to_all x2, waiting for transfers between devices: 18.7 us -> 8.19 us  [to_experts(): lax.all_to_all(found, 'exp', split_axis=0, concat_axis=0, tiled=True)]
    ppermute x5, waiting for transfers between devices: 18.2 us -> 27.5 us  [swapped(): return lax.ppermute(block, 'ctx', [(0, 1), (1, 0)])]
    all_to_all x0 -> x1, starting transfers between devices: none -> 5.4 us  [local(): lax.all_to_all(back.reshape(experts, channels, capacity), 'exp', split_ax...]
    all_to_all x0 -> x1, waiting for transfers between devices: none -> 3.29 us  [local(): lax.all_to_all(back.reshape(experts, channels, capacity), 'exp', split_ax...]
  transfers between devices with their start and end apart: 9 -> 8, of which waited for: 7 -> 6; matrix products, arithmetic and copies ran while one was open for 12% -> 15% of each run, Pallas kernels for 0% -> 0%
where the time goes in v2:
time: 126 us; the launch traced here: 125 us
  waiting for transfers between devices  39 us (31%)
  matrix products  28.5 us (23%)
  Pallas kernels  26.8 us (21%)
  starting transfers between devices  21.7 us (17%)
  local copies, waits for them, and re-layouts  4.04 us (3%)
  other arithmetic  3.93 us (3%)
    dot_general x14, matrix products, product(): lax.dot_general(left, right, (dims, ((), ())), preferred_element_type=F32)  28.5 us
    ppermute x5, waiting for transfers between devices, swapped(): return lax.ppermute(block, 'ctx', [(0, 1), (1, 0)])  27.5 us
    pallas_call x1, Pallas kernels, gathered(): pl.pallas_call(gather_kernel, out_shape=jax.ShapeDtypeStruct((size,) + ce...  26.8 us
    all_to_all x2, starting transfers between devices, to_experts(): lax.all_to_all(found, 'exp', split_axis=0, concat_axis=0, tiled=True)  10.9 us
    all_to_all x2, waiting for transfers between devices, to_experts(): lax.all_to_all(found, 'exp', split_axis=0, concat_axis=0, tiled=True)  8.19 us
    ppermute x5, starting transfers between devices, swapped(): return lax.ppermute(block, 'ctx', [(0, 1), (1, 0)])  5.42 us
    all_to_all x1, starting transfers between devices, local(): lax.all_to_all(back.reshape(experts, channels, capacity), 'exp', split_ax...  5.4 us
    all_to_all x1, waiting for transfers between devices, local(): lax.all_to_all(back.reshape(experts, channels, capacity), 'exp', split_ax...  3.29 us
  transfers between devices with their start and end apart: 8, of which 6 were waited for; matrix products, arithmetic and copies ran while one was open for 15% of the time, Pallas kernels for 0%

profile of v2, /device:TPU:0, one launch (start us, length us, event | category | flops | bytes accessed | tf_op | source)
XLA Modules:
  0.0 125.0 jit_solution(14080150489101892875)
XLA Ops:
  0.6 0.0 copy-start
  0.6 0.8 fusion.122
  1.4 0.2 select_reduce_fusion.1
  1.6 0.8 multiply_add_fusion.2
  2.4 0.0 copy-start.6
  2.4 0.0 copy-start.4
  2.4 2.2 %fusion.45 = bf16[12,16,8,128]{3,2,1,0:T(8,128)(2,1)S(1)} fusion(s32[512]{0:T(512)S(1)} %bitcast.136, s32[512]{0:T(512)S(1)} %bitcast.133, bf16[96,512]{1,0:T(8,128)(2,1)} %param.9, bf16[96,512]{1,0:T(8,128)(2,1)} %param.8), kind=kOutput, calls=%fused_computation.47 | convolution fusion | flops 210501632 | bytes 593920 | tf_op jit(solution)/shard_map/dot_general | solution.py:26
  4.6 0.8 copy.27
  5.4 7.4 %all-to-all-start.1 = ((bf16[16,96,128]{2,1,0:T(8,128)(2,1)}), bf16[16,96,128]{2,1,0:T(8,128)(2,1)S(1)}, u32[]{:S(2)}, u32[]{:S(2)}) async-start(bf16[16,96,128]{2,1,0:T(8,128)(2,1)} %bitcast.112), calls=%async_computation.1 | async-start | bytes 786432 | tf_op jit(solution)/shard_map/all_to_all | solution.py:176
  12.8 0.0 copy-done.6
  12.8 0.0 copy-done.4
  12.9 1.7 %fusion.14 = (bf16[2048,512]{1,0:T(8,128)(2,1)S(1)}, bf16[2048,512]{1,0:T(8,128)(2,1)S(1)}) fusion(s32[512]{0:T(512)S(1)} %bitcast.134, s32[512]{0:T(512)S(1)} %bitcast.137), kind=kLoop, calls=%fused_computation.18 | loop fusion | flops 4194304 | bytes 4198400 | tf_op jit(solution)/shard_map/convert_element_type | solution.py:161
  14.6 0.0 copy-start.3
  14.6 1.4 %fusion.46 = bf16[12,16,8,128]{3,2,1,0:T(8,128)(2,1)S(1)} fusion(bf16[2048,512]{1,0:T(8,128)(2,1)S(1)} %get-tuple-element.21, bf16[2048,512]{1,0:T(8,128)(2,1)S(1)} %get-tuple-element.20, bf16[96,512]{1,0:T(8,128)(2,1)S(1)} %get-tuple-element.11, bf16[96,512]{1,0:T(8,128)(2,1)S(1)} %get-tuple-element.10), kind=kOutput, calls=%fused_computation.48 | convolution fusion | flops 411631616 | bytes 4784128 | tf_op jit(solution)/shard_map/dot_general | solution.py:26
  16.0 0.8 copy.28
  16.8 8.2 %all-to-all-done.1 = bf16[16,96,128]{2,1,0:T(8,128)(2,1)S(1)} async-done(((bf16[16,96,128]{2,1,0:T(8,128)(2,1)}), bf16[16,96,128]{2,1,0:T(8,128)(2,1)S(1)}, u32[]{:S(2)}, u32[]{:S(2)}) %all-to-all-start.1) | async-done | bytes 393248 | tf_op jit(solution)/shard_map/all_to_all | solution.py:176
  25.0 3.6 %all-to-all-start = ((bf16[16,96,128]{2,1,0:T(8,128)(2,1)}), bf16[16,96,128]{2,1,0:T(8,128)(2,1)S(1)}, u32[]{:S(2)}, u32[]{:S(2)}) async-start(bf16[16,96,128]{2,1,0:T(8,128)(2,1)} %bitcast.114), calls=%async_computation | async-start | bytes 786432 | tf_op jit(solution)/shard_map/all_to_all | solution.py:176
  28.6 1.6 %collective-permute-start.1 = (bf16[1536,128]{1,0:T(8,128)(2,1)S(1)}, bf16[1536,128]{1,0:T(8,128)(2,1)S(1)}, u32[]{:S(2)}, u32[]{:S(2)}) collective-permute-start(bf16[1536,128]{1,0:T(8,128)(2,1)S(1)} %bitcast.125), channel_id=1, source_target_pairs={{0,16},{16,0},{1,17},{17,1},{2,18},{18,2},{3,19},{19,3},{4,20},{20... | collective-permute-start | bytes 1179656 | tf_op jit(solution)/shard_map/ppermute | solution.py:30
  30.2 0.0 copy-done.3
  30.2 0.5 collective-permute-start.4
  30.7 11.4 %collective-permute-done.4 = bf16[96,512]{1,0:T(8,128)(2,1)S(1)} collective-permute-done((bf16[96,512]{1,0:T(8,128)(2,1)S(1)}, bf16[96,512]{1,0:T(8,128)(2,1)S(1)}, u32[]{:S(2)}, u32[]{:S(2)}) %collective-permute-start.4) | collective-permute-done | bytes 98336 | tf_op jit(solution)/shard_map/ppermute | solution.py:30
  42.1 0.0 all-to-all-done
  42.1 0.0 copy-start.1
  42.1 1.6 %collective-permute-start = (bf16[1536,128]{1,0:T(8,128)(2,1)S(1)}, bf16[1536,128]{1,0:T(8,128)(2,1)S(1)}, u32[]{:S(2)}, u32[]{:S(2)}) collective-permute-start(bf16[1536,128]{1,0:T(8,128)(2,1)S(1)} %bitcast.128), channel_id=1, source_target_pairs={{0,16},{16,0},{1,17},{17,1},{2,18},{18,2},{3,19},{19,3},{4,20},{20... | collective-permute-start | bytes 1179656 | tf_op jit(solution)/shard_map/ppermute | solution.py:30
  43.7 0.0 collective-permute-done.1
  43.7 3.9 %fusion.22 = f32[1536,256]{0,1:T(8,128)S(1)} fusion(bf16[1,1536,1536]{2,1,0:T(8,128)(2,1)} %param.14, bf16[1536,128]{1,0:T(8,128)(2,1)S(1)} %collective-permute-done.1, bf16[1536,128]{1,0:T(8,128)(2,1)S(1)} %bitcast.126), kind=kOutput, calls=%fused_computation.22 | convolution fusion | flops 1209532416 | bytes 7077888 | tf_op jit(solution)/shard_map/dot_general | solution.py:26
  47.6 0.0 copy-start.11
  47.7 0.0 slice-start.1
  47.7 5.0 %collective-permute-done = bf16[1536,128]{1,0:T(8,128)(2,1)S(1)} collective-permute-done((bf16[1536,128]{1,0:T(8,128)(2,1)S(1)}, bf16[1536,128]{1,0:T(8,128)(2,1)S(1)}, u32[]{:S(2)}, u32[]{:S(2)}) %collective-permute-start) | collective-permute-done | bytes 393248 | tf_op jit(solution)/shard_map/ppermute | solution.py:30
  52.7 0.0 copy-done.1
  52.7 4.5 %fusion.25 = bf16[1536,256]{0,1:T(8,128)(2,1)S(1)} fusion(bf16[1,1536,1536]{2,1,0:T(8,128)(2,1)} %param.15, f32[1536,256]{0,1:T(8,128)S(1)} %fusion.22, bf16[1536,128]{1,0:T(8,128)(2,1)S(1)} %collective-permute-done, bf16[1536,128]{1,0:T(8,128)(2,1)S(1)} %bitcast.129), kind=kOutput, calls=%fused_computation.23 | convolution fusion | flops 1217003520 | bytes 7864320 | tf_op jit(solution)/shard_map/dot_general | solution.py:26
  57.2 0.0 copy-done.7
  57.3 0.0 copy-done.11
  57.3 0.0 copy-done.8
  57.3 0.0 slice-done
  57.3 0.0 slice-done.1
  57.3 1.6 %fusion.37 = bf16[1536,128]{0,1:T(8,128)(2,1)S(1)} fusion(bf16[1,1536,1536]{2,1,0:T(8,128)(2,1)S(1)} %bitcast.118, bf16[1536,256]{0,1:T(8,128)(2,1)S(1)} %fusion.25), kind=kOutput, calls=%fused_computation.30 | convolution fusion | flops 604176384 | bytes 5505024 | tf_op jit(solution)/shard_map/dot_general | solution.py:26
  58.9 1.6 %collective-permute-start.2 = (bf16[1536,128]{0,1:T(8,128)(2,1)S(1)}, bf16[1536,128]{0,1:T(8,128)(2,1)S(1)}, u32[]{:S(2)}, u32[]{:S(2)}) collective-permute-start(bf16[1536,128]{0,1:T(8,128)(2,1)S(1)} %fusion.37), channel_id=1, source_target_pairs={{0,16},{16,0},{1,17},{17,1},{2,18},{18,2},{3,19},{19,3},{4,20},{20... | collective-permute-start | bytes 1179656 | tf_op jit(solution)/shard_map/ppermute | solution.py:30
  60.5 0.1 slice_dynamic-update-slice_fusion.3
  60.7 0.1 slice_dynamic-update-slice_fusion.2
  60.8 7.8 %collective-permute-done.2 = bf16[1536,128]{0,1:T(8,128)(2,1)S(1)} collective-permute-done((bf16[1536,128]{0,1:T(8,128)(2,1)S(1)}, bf16[1536,128]{0,1:T(8,128)(2,1)S(1)}, u32[]{:S(2)}, u32[]{:S(2)}) %collective-permute-start.2) | collective-permute-done | bytes 393248 | tf_op jit(solution)/shard_map/ppermute | solution.py:30
  68.6 1.7 %add_convert_fusion = bf16[1536,128]{0,1:T(8,128)(2,1)S(1)} fusion(bf16[1536,128]{0,1:T(8,128)(2,1)S(1)} %collective-permute-done.2, bf16[1,1536,1536]{2,1,0:T(8,128)(2,1)S(1)} %bitcast.118, bf16[1536,256]{0,1:T(8,128)(2,1)S(1)} %fusion.25), kind=kOutput, calls=%fused_computation.54 | convolution fusion | flops 604569600 | bytes 5898240 | tf_op jit(solution)/shard_map/dot_general | solution.py:26
  70.3 0.9 copy.14
  71.2 5.4 %all-to-all-start.2 = ((bf16[16,96,128]{2,1,0:T(8,128)(2,1)}), bf16[16,96,128]{2,1,0:T(8,128)(2,1)S(1)}, u32[]{:S(2)}, u32[]{:S(2)}) async-start(bf16[16,96,128]{2,1,0:T(8,128)(2,1)} %bitcast.20), calls=%async_computation.2 | async-start | bytes 786432 | tf_op jit(solution)/shard_map/all_to_all | solution.py:201
  76.6 0.1 slice_dynamic-update-slice_fusion.1
  76.7 0.1 slice_dynamic-update-slice_fusion
  76.9 0.0 copy-start.12
  76.9 4.7 %fusion = bf16[1,1536,1536]{2,1,0:T(8,128)(2,1)} fusion(bf16[1536,256]{0,1:T(8,128)(2,1)S(1)} %fusion.25, bf16[1536,128]{1,0:T(8,128)(2,1)} %copy-done.7, bf16[1536,128]{1,0:T(8,128)(2,1)S(1)} %bitcast.127), kind=kOutput, calls=%fused_computation.2 | convolution fusion | flops 1211891712 | bytes 6291456 | tf_op jit(solution)/shard_map/dot_general | solution.py:26
  81.6 0.0 copy-start.5
  81.6 0.0 copy-start.10
  81.6 3.8 %fusion.1 = bf16[1,1536,1536]{2,1,0:T(8,128)(2,1)} fusion(f32[1536,256]{0,1:T(8,128)S(1)} %copy-done.12, bf16[1536,128]{1,0:T(8,128)(2,1)S(1)} %copy-done.9, bf16[1536,128]{1,0:T(8,128)(2,1)S(1)} %bitcast.130), kind=kOutput, calls=%fused_computation.3 | convolution fusion | flops 1215430656 | bytes 7077888 | tf_op jit(solution)/shard_map/dot_general | solution.py:26
  85.5 3.3 %all-to-all-done.2 = bf16[16,96,128]{2,1,0:T(8,128)(2,1)S(1)} async-done(((bf16[16,96,128]{2,1,0:T(8,128)(2,1)}), bf16[16,96,128]{2,1,0:T(8,128)(2,1)S(1)}, u32[]{:S(2)}, u32[]{:S(2)}) %all-to-all-start.2) | async-done | bytes 393248 | tf_op jit(solution)/shard_map/all_to_all | solution.py:201
  88.8 1.1 fusion.86
  89.9 26.8 %shard_map.111 = bf16[16,96,512]{2,1,0:T(8,128)(2,1)S(1)} custom-call(bf16[96,512]{1,0:T(8,128)(2,1)S(1)} %get-tuple-element.18.cells), custom_call_target="tpu_custom_call" | custom-call | tf_op jit(solution)/shard_map/pallas_call | solution.py:120
  116.7 0.1 fusion.120
  116.8 0.5 convolution_bitcast_fusion
  117.4 0.5 convolution_bitcast_fusion.1
  117.9 0.6 fusion.60
  118.5 0.2 pad_maximum_fusion
  118.7 0.5 fusion.66
  119.2 0.2 collective-permute-start.3
  119.4 1.7 %convolution_add_fusion = f32[480,768]{1,0:T(8,128)} fusion(f32[480,768]{1,0:T(8,128)S(1)} %fusion.60, bf16[768,512]{1,0:T(8,128)(2,1)S(1)} %bitcast.121, bf16[480,1024]{1,0:T(8,128)(2,1)S(1)} %slice_dynamic-update-slice_fusion), kind=kOutput, calls=%fused_computation.44 | convolution fusion | flops 377856000 | bytes 4227072 | tf_op jit(solution)/shard_map/dot_general | solution.py:26
  121.1 3.3 %collective-permute-done.3 = bf16[96,512]{1,0:T(8,128)(2,1)S(1)} collective-permute-done((bf16[96,512]{1,0:T(8,128)(2,1)S(1)}, bf16[96,512]{1,0:T(8,128)(2,1)S(1)}, u32[]{:S(2)}, u32[]{:S(2)}) %collective-permute-start.3) | collective-permute-done | bytes 98336 | tf_op jit(solution)/shard_map/ppermute | solution.py:30
  124.3 0.7 add_convert_fusion.1
  (20 shorter events, 0.1 us)
Async XLA Ops:
  0.6 116.2 %copy-start = (bf16[5,96,768]{2,1,0:T(8,128)(2,1)S(1)}, bf16[5,96,768]{2,1,0:T(8,128)(2,1)}, u32[]{:S(2)}) copy-start(bf16[5,96,768]{2,1,0:T(8,128)(2,1)} %param.11) | copy-start | bytes 2211844
  2.4 10.4 %copy-start.6 = (f32[512,2]{0,1:T(2,128)S(1)}, f32[512,2]{0,1:T(2,128)}, u32[]{:S(2)}) copy-start(f32[512,2]{0,1:T(2,128)} %param.13) | copy-start | bytes 12292
  2.4 10.4 %copy-start.4 = (bf16[96,512]{1,0:T(8,128)(2,1)S(1)}, bf16[96,512]{1,0:T(8,128)(2,1)}, u32[]{:S(2)}) copy-start(bf16[96,512]{1,0:T(8,128)(2,1)} %param.10) | copy-start | bytes 294916
  5.4 19.6 %all-to-all-start.1 = ((bf16[16,96,128]{2,1,0:T(8,128)(2,1)}), bf16[16,96,128]{2,1,0:T(8,128)(2,1)S(1)}, u32[]{:S(2)}, u32[]{:S(2)}) async-start(bf16[16,96,128]{2,1,0:T(8,128)(2,1)} %bitcast.112), calls=%async_computation.1 | async-start | bytes 786432 | tf_op jit(solution)/shard_map/all_to_all | solution.py:176
  14.6 15.6 %copy-start.3 = (bf16[96,512]{1,0:T(8,128)(2,1)S(1)}, bf16[96,512]{1,0:T(8,128)(2,1)}, u32[]{:S(2)}) copy-start(bf16[96,512]{1,0:T(8,128)(2,1)} %param.8) | copy-start | bytes 294916
  25.0 17.1 %all-to-all-start = ((bf16[16,96,128]{2,1,0:T(8,128)(2,1)}), bf16[16,96,128]{2,1,0:T(8,128)(2,1)S(1)}, u32[]{:S(2)}, u32[]{:S(2)}) async-start(bf16[16,96,128]{2,1,0:T(8,128)(2,1)} %bitcast.114), calls=%async_computation | async-start | bytes 786432 | tf_op jit(solution)/shard_map/all_to_all | solution.py:176
  28.6 15.1 %collective-permute-start.1 = (bf16[1536,128]{1,0:T(8,128)(2,1)S(1)}, bf16[1536,128]{1,0:T(8,128)(2,1)S(1)}, u32[]{:S(2)}, u32[]{:S(2)}) collective-permute-start(bf16[1536,128]{1,0:T(8,128)(2,1)S(1)} %bitcast.125), channel_id=1, source_target_pairs={{0,16},{16,0},{1,17},{17,1},{2,18},{18,2},{3,19},{19,3},{4,20},{20... | collective-permute-start | bytes 1179656 | tf_op jit(solution)/shard_map/ppermute | solution.py:30
  30.2 11.9 %collective-permute-start.4 = (bf16[96,512]{1,0:T(8,128)(2,1)S(1)}, bf16[96,512]{1,0:T(8,128)(2,1)S(1)}, u32[]{:S(2)}, u32[]{:S(2)}) collective-permute-start(bf16[96,512]{1,0:T(8,128)(2,1)S(1)} %copy-done.3), channel_id=1, source_target_pairs={{0,16},{16,0},{1,17},{17,1},{2,18},{18,2},{3,19},{19,3},{4,20},{20... | collective-permute-start | bytes 294920 | tf_op jit(solution)/shard_map/ppermute | solution.py:30
  42.1 10.6 %copy-start.1 = (bf16[16,96,128]{2,1,0:T(8,128)(2,1)}, bf16[16,96,128]{2,1,0:T(8,128)(2,1)S(1)}, u32[]{:S(2)}) copy-start(bf16[16,96,128]{2,1,0:T(8,128)(2,1)S(1)} %all-to-all-done) | copy-start | bytes 1179652
  42.1 10.6 %collective-permute-start = (bf16[1536,128]{1,0:T(8,128)(2,1)S(1)}, bf16[1536,128]{1,0:T(8,128)(2,1)S(1)}, u32[]{:S(2)}, u32[]{:S(2)}) collective-permute-start(bf16[1536,128]{1,0:T(8,128)(2,1)S(1)} %bitcast.128), channel_id=1, source_target_pairs={{0,16},{16,0},{1,17},{17,1},{2,18},{18,2},{3,19},{19,3},{4,20},{20... | collective-permute-start | bytes 1179656 | tf_op jit(solution)/shard_map/ppermute | solution.py:30
  43.7 13.5 %copy-start.7 = (bf16[1536,128]{1,0:T(8,128)(2,1)}, bf16[1536,128]{1,0:T(8,128)(2,1)S(1)}, u32[]{:S(2)}) copy-start(bf16[1536,128]{1,0:T(8,128)(2,1)S(1)} %collective-permute-done.1) | copy-start | bytes 1179652
  43.7 13.6 %slice-start = ((s8[4718592]{0:T(1024)(128)(4,1)}), s8[4194304]{0:T(1024)(128)(4,1)S(1)}, s32[]{:S(2)}) async-start(s8[4718592]{0:T(1024)(128)(4,1)} %bitcast.117), calls=%async_computation.3 | async-start | bytes 8388608
  47.6 9.6 %copy-start.11 = (f32[1536,256]{0,1:T(8,128)}, f32[1536,256]{0,1:T(8,128)S(1)}, u32[]{:S(2)}) copy-start(f32[1536,256]{0,1:T(8,128)S(1)} %fusion.22) | copy-start | bytes 4718596
  47.7 9.6 %slice-start.1 = ((s8[4718592]{0:T(1024)(128)(4,1)}), s8[524288]{0:T(1024)(128)(4,1)S(1)}, s32[]{:S(2)}) async-start(s8[4718592]{0:T(1024)(128)(4,1)} %bitcast.117), calls=%async_computation.4 | async-start | bytes 1048576
  52.7 4.6 %copy-start.8 = (bf16[1536,128]{1,0:T(8,128)(2,1)}, bf16[1536,128]{1,0:T(8,128)(2,1)S(1)}, u32[]{:S(2)}) copy-start(bf16[1536,128]{1,0:T(8,128)(2,1)S(1)} %collective-permute-done) | copy-start | bytes 1179652
  58.9 9.7 %collective-permute-start.2 = (bf16[1536,128]{0,1:T(8,128)(2,1)S(1)}, bf16[1536,128]{0,1:T(8,128)(2,1)S(1)}, u32[]{:S(2)}, u32[]{:S(2)}) collective-permute-start(bf16[1536,128]{0,1:T(8,128)(2,1)S(1)} %fusion.37), channel_id=1, source_target_pairs={{0,16},{16,0},{1,17},{17,1},{2,18},{18,2},{3,19},{19,3},{4,20},{20... | collective-permute-start | bytes 1179656 | tf_op jit(solution)/shard_map/ppermute | solution.py:30
  71.2 17.6 %all-to-all-start.2 = ((bf16[16,96,128]{2,1,0:T(8,128)(2,1)}), bf16[16,96,128]{2,1,0:T(8,128)(2,1)S(1)}, u32[]{:S(2)}, u32[]{:S(2)}) async-start(bf16[16,96,128]{2,1,0:T(8,128)(2,1)} %bitcast.20), calls=%async_computation.2 | async-start | bytes 786432 | tf_op jit(solution)/shard_map/all_to_all | solution.py:201
  76.8 4.8 %copy-start.2 = (bf16[16,96,128]{2,1,0:T(8,128)(2,1)S(1)}, bf16[16,96,128]{2,1,0:T(8,128)(2,1)}, u32[]{:S(2)}) copy-start(bf16[16,96,128]{2,1,0:T(8,128)(2,1)} %copy-done.1) | copy-start | bytes 1179652
  76.9 4.8 %copy-start.9 = (bf16[1536,128]{1,0:T(8,128)(2,1)S(1)}, bf16[1536,128]{1,0:T(8,128)(2,1)}, u32[]{:S(2)}) copy-start(bf16[1536,128]{1,0:T(8,128)(2,1)} %copy-done.8) | copy-start | bytes 1179652
  76.9 4.7 %copy-start.12 = (f32[1536,256]{0,1:T(8,128)S(1)}, f32[1536,256]{0,1:T(8,128)}, u32[]{:S(2)}) copy-start(f32[1536,256]{0,1:T(8,128)} %copy-done.11) | copy-start | bytes 4718596
  81.6 7.2 %copy-start.5 = (bf16[96,512]{1,0:T(8,128)(2,1)S(1)}, bf16[96,512]{1,0:T(8,128)(2,1)}, u32[]{:S(2)}) copy-start(bf16[96,512]{1,0:T(8,128)(2,1)} %param.10) | copy-start | bytes 294916
  81.6 7.2 %copy-start.10 = (bf16[96,512]{1,0:T(8,128)(2,1)S(1)}, bf16[96,512]{1,0:T(8,128)(2,1)}, u32[]{:S(2)}) copy-start(bf16[96,512]{1,0:T(8,128)(2,1)} %param.9) | copy-start | bytes 294916
  119.2 5.1 %collective-permute-start.3 = (bf16[96,512]{1,0:T(8,128)(2,1)S(1)}, bf16[96,512]{1,0:T(8,128)(2,1)S(1)}, u32[]{:S(2)}, u32[]{:S(2)}) collective-permute-start(bf16[96,512]{1,0:T(8,128)(2,1)S(1)} %select_convert_fusion), channel_id=1, source_target_pairs={{0,16},{16,0},{1,17},{17,1},{2,18},{18,2},{3,19},{19,3},{4,20},{20... | collective-permute-start | bytes 294920 | tf_op jit(solution)/shard_map/ppermute | solution.py:30

commit v3 on v2

--- a/solution.py
+++ b/solution.py
@@ -137,6 +137,63 @@
     )(cells)
 
 
+def spread_kernel(cells, out, a_sent, a_got, y_sent, y_got):
+    c, e = lax.axis_index("ctx"), lax.axis_index("exp")
+    size = cells.shape[0]
+    other = (1 - c, e)
+
+    def to(d):
+        return lax.rem(e + d, size)
+
+    def source(d):
+        return lax.rem(e + size - d, size)
+
+    barrier = pltpu.get_barrier_semaphore()
+    greet(barrier, [(c, to(d)) for d in range(1, size)] + [other])
+    pl.semaphore_wait(barrier, size)
+
+    def sending(d):
+        return remote(cells.at[to(d)], out.at[0, e], a_sent.at[d], a_got.at[d], (c, to(d)))
+
+    def arriving(d):
+        slot = source(d)
+        return remote(cells.at[slot], out.at[0, slot], a_sent.at[d], a_got.at[d], (c, slot))
+
+    def handing(d):
+        slot = source(d)
+        return remote(out.at[0, slot], out.at[1, slot], y_sent.at[d], y_got.at[d], other)
+
+    mine = remote(cells.at[e], out.at[1, e], y_sent.at[0], y_got.at[0], other)
+    mine.start()
+    for d in range(1, size):
+        sending(d).start()
+    kept = pltpu.make_async_copy(cells.at[e], out.at[0, e], a_sent.at[0])
+    kept.start()
+    for d in range(1, size):
+        arriving(d).wait_recv()
+        handing(d).start()
+    kept.wait()
+    mine.wait()
+    for d in range(1, size):
+        handing(d).wait()
+        sending(d).wait_send()
+
+
+def spread_rows(cells):
+    size = cells.shape[0]
+    dma = pltpu.SemaphoreType.DMA
+    return pl.pallas_call(
+        spread_kernel,
+        out_shape=jax.ShapeDtypeStruct((2,) + cells.shape, cells.dtype),
+        in_specs=[pl.BlockSpec(memory_space=pltpu.VMEM)],
+        out_specs=pl.BlockSpec(memory_space=pltpu.VMEM),
+        scratch_shapes=[dma((size,)), dma((size,)), dma((size,)), dma((size,))],
+        compiler_params=pltpu.CompilerParams(
+            collective_id=1, has_side_effects=True, vmem_limit_bytes=24 * 2**20
+        ),
+    )(cells)
+
+
 def local(inputs, pre_act, grad_out, conv_weight, expert_ids, gate_values, expert_in, expert_out):
     channels, bins = inputs.shape
     experts = lax.axis_size("exp")
@@ -170,17 +227,28 @@
         [(grad_float * gates[k][None, :]).astype(BF16) for k in range(len(picks))], axis=1
     )
 
-    def to_experts(cells, pick):
+    def picked(cells, pick):
         found = product(cells, pick, ((1,), (1,))).astype(BF16)
-        found = found.reshape(channels, experts, capacity).transpose(1, 0, 2)
+        return found.reshape(channels, experts, capacity).transpose(1, 0, 2)
+
+    def to_experts(found):
         found = lax.all_to_all(found, "exp", split_axis=0, concat_axis=0, tiled=True)
         found = found.reshape(width, capacity)
         if pair:
             return jnp.concatenate([found, swapped(found)], axis=1)
         return lax.all_gather(found, "ctx", axis=1, tiled=True)
 
-    rows_in = to_experts(activated, pick_any)
-    rows_grad = to_experts(gated, pick_each)
+    sent_in = picked(activated, pick_any)
+    sent_grad = picked(gated, pick_each)
+    if pair and experts == 16:
+        both = spread_rows(jnp.concatenate([sent_in, sent_grad], axis=1))
+        rows_in, rows_grad = [
+            jnp.concatenate([half[0].reshape(width, -1), half[1].reshape(width, -1)], axis=1)
+            for half in (both[:, :, :channels], both[:, :, channels:])
+        ]
+    else:
+        rows_in = to_experts(sent_in)
+        rows_grad = to_experts(sent_grad)
 
     first = expert_in[0]
     second = expert_out[0]

time: 126 us -> 117 us (0.929)
  Pallas kernels: 26.8 us -> 55.6 us
  waiting for transfers between devices: 39 us -> 15.2 us
  starting transfers between devices: 21.7 us -> 13.2 us
  matrix products: 28.5 us -> 23.7 us
    pallas_call x0 -> x1, Pallas kernels: none -> 28.8 us  [spread_rows(): pl.pallas_call(spread_kernel, out_shape=jax.ShapeDtypeStruct((2,) + cells...]
    ppermute x5 -> x3, waiting for transfers between devices: 27.5 us -> 3.6 us  [swapped(): return lax.ppermute(block, 'ctx', [(0, 1), (1, 0)])]
    all_to_all x2 -> x0, starting transfers between devices: 10.9 us -> none  [to_experts(): lax.all_to_all(found, 'exp', split_axis=0, concat_axis=0, tiled=True)]
    all_to_all x1, waiting for transfers between devices: 3.29 us -> 11.6 us  [local(): lax.all_to_all(back.reshape(experts, channels, capacity), 'exp', split_ax...]
    all_to_all x2 -> x0, waiting for transfers between devices: 8.19 us -> none  [to_experts(): lax.all_to_all(found, 'exp', split_axis=0, concat_axis=0, tiled=True)]
    dot_general x14, matrix products: 28.5 us -> 23.7 us  [product(): lax.dot_general(left, right, (dims, ((), ())), preferred_element_type=F32)]
    all_to_all x1, starting transfers between devices: 5.4 us -> 7.91 us  [local(): lax.all_to_all(back.reshape(experts, channels, capacity), 'exp', split_ax...]
    reshape x2, local copies, waits for them, and re-layouts: 1.63 us -> 0.14 us  [picked(): return found.reshape(channels, experts, capacity).transpose(1, 0, 2)]
  transfers between devices with their start and end apart: 8 -> 4, of which waited for: 6 -> 3; matrix products, arithmetic and copies ran while one was open for 15% -> 23% of each run, Pallas kernels for 0% -> 25%
where the time goes in v3:
time: 117 us
  Pallas kernels  55.6 us (48%)
  matrix products  23.7 us (20%)
  waiting for transfers between devices  15.2 us (13%)
  starting transfers between devices  13.2 us (11%)
  local copies, waits for them, and re-layouts  4.15 us (4%)
  other arithmetic  4.01 us (3%)
    pallas_call x1, Pallas kernels, spread_rows(): pl.pallas_call(spread_kernel, out_shape=jax.ShapeDtypeStruct((2,) + cells...  28.8 us
    pallas_call x1, Pallas kernels, gathered(): pl.pallas_call(gather_kernel, out_shape=jax.ShapeDtypeStruct((size,) + ce...  26.8 us
    dot_general x14, matrix products, product(): lax.dot_general(left, right, (dims, ((), ())), preferred_element_type=F32)  23.7 us
    all_to_all x1, waiting for transfers between devices, local(): lax.all_to_all(back.reshape(experts, channels, capacity), 'exp', split_ax...  11.6 us
    all_to_all x1, starting transfers between devices, local(): lax.all_to_all(back.reshape(experts, channels, capacity), 'exp', split_ax...  7.91 us
    ppermute x3, starting transfers between devices, swapped(): return lax.ppermute(block, 'ctx', [(0, 1), (1, 0)])  5.24 us
    ppermute x3, waiting for transfers between devices, swapped(): return lax.ppermute(block, 'ctx', [(0, 1), (1, 0)])  3.6 us
  transfers between devices with their start and end apart: 4, of which 3 were waited for; matrix products, arithmetic and copies ran while one was open for 23% of the time, Pallas kernels for 25%

profile of v3, /device:TPU:0, one launch (start us, length us, event | category | flops | bytes accessed | tf_op | source)
XLA Modules:
  0.0 116.8 jit_solution(10922915582196467884)
XLA Ops:
  0.6 0.0 copy-start
  0.6 3.0 %collective-permute-start.2 = (bf16[96,512]{1,0:T(8,128)(2,1)}, bf16[96,512]{1,0:T(8,128)(2,1)S(1)}, u32[]{:S(2)}, u32[]{:S(2)}) collective-permute-start(bf16[96,512]{1,0:T(8,128)(2,1)} %param.8), channel_id=1, source_target_pairs={{0,16},{16,0},{1,17},{17,1},{2,18},{18,2},{3,19},{19,3},{4,20},{20... | collective-permute-start | bytes 294920 | tf_op jit(solution)/shard_map/ppermute | solution.py:30
  3.7 0.8 fusion.123
  4.4 0.2 select_reduce_fusion.1
  4.7 0.8 fusion.122
  5.4 0.8 multiply_add_fusion.2
  6.2 0.0 copy-start.1
  6.2 0.0 copy-start.3
  6.2 1.7 %fusion.14 = (bf16[2048,512]{1,0:T(8,128)(2,1)S(1)}, bf16[2048,512]{1,0:T(8,128)(2,1)S(1)}) fusion(s32[512]{0:T(512)S(1)} %bitcast.141, s32[512]{0:T(512)S(1)} %bitcast.144), kind=kLoop, calls=%fused_computation.18 | loop fusion | flops 4194304 | bytes 4198400 | tf_op jit(solution)/shard_map/convert_element_type | solution.py:218
  7.9 0.0 copy-done.1
  8.0 0.0 copy-done.3
  8.0 0.0 copy-start.2
  8.0 1.2 %fusion.45 = bf16[12,16,8,128]{3,2,1,0:T(8,128)(2,1)S(1)} fusion(s32[512]{0:T(512)S(1)} %bitcast.145, s32[512]{0:T(512)S(1)} %bitcast.142, bf16[96,512]{1,0:T(8,128)(2,1)S(1)} %copy-done.3, bf16[96,512]{1,0:T(8,128)(2,1)S(1)} %copy-done.1), kind=kOutput, calls=%fused_computation.47 | convolution fusion | flops 210501632 | bytes 593920 | tf_op jit(solution)/shard_map/dot_general | solution.py:26
  9.2 0.1 copy.28
  9.3 0.0 copy-done.2
  9.3 0.0 slice-start
  9.3 1.4 %fusion.46 = bf16[12,16,8,128]{3,2,1,0:T(8,128)(2,1)S(1)} fusion(bf16[2048,512]{1,0:T(8,128)(2,1)S(1)} %get-tuple-element.25, bf16[2048,512]{1,0:T(8,128)(2,1)S(1)} %get-tuple-element.24, bf16[96,512]{1,0:T(8,128)(2,1)S(1)} %get-tuple-element.15, bf16[96,512]{1,0:T(8,128)(2,1)S(1)} %get-tuple-element.14), kind=kOutput, calls=%fused_computation.48 | convolution fusion | flops 411631616 | bytes 4784128 | tf_op jit(solution)/shard_map/dot_general | solution.py:26
  10.7 0.0 slice-start.1
  10.7 0.1 copy.27
  10.8 0.1 pad_maximum_fusion.1.cells
  10.9 28.8 %shard_map.111 = bf16[2,16,192,128]{3,2,1,0:T(8,128)(2,1)S(1)} custom-call(bf16[16,192,128]{2,1,0:T(8,128)(2,1)S(1)} %pad_maximum_fusion.1.cells), custom_call_target="tpu_custom_call" | custom-call | tf_op jit(solution)/shard_map/pallas_call | solution.py:185
  39.7 0.0 slice-start.4
  39.7 0.1 fusion.121
  39.8 0.0 slice-done
  39.8 0.0 slice-done.1
  39.8 0.0 slice-start.5
  39.8 1.4 %fusion.22 = f32[1536,256]{0,1:T(8,128)S(1)} fusion(bf16[1,1536,1536]{2,1,0:T(8,128)(2,1)S(1)} %bitcast.120, bf16[1536,128]{1,0:T(8,128)(2,1)S(1)} %bitcast.135, bf16[1536,128]{1,0:T(8,128)(2,1)S(1)} %bitcast.137), kind=kOutput, calls=%fused_computation.22 | convolution fusion | flops 1209532416 | bytes 7077888 | tf_op jit(solution)/shard_map/dot_general | solution.py:26
  41.2 0.0 copy-start.5
  41.3 0.6 slice-done.4
  41.9 0.1 slice-done.5
  42.0 2.1 %fusion.25 = bf16[1536,256]{0,1:T(8,128)(2,1)S(1)} fusion(bf16[1,1536,1536]{2,1,0:T(8,128)(2,1)S(1)} %bitcast.155, f32[1536,256]{0,1:T(8,128)S(1)} %fusion.22, bf16[1536,128]{1,0:T(8,128)(2,1)S(1)} %bitcast.133, bf16[1536,128]{1,0:T(8,128)(2,1)S(1)} %bitcast.131), kind=kOutput, calls=%fused_computation.23 | convolution fusion | flops 1217003520 | bytes 7864320 | tf_op jit(solution)/shard_map/dot_general | solution.py:26
  44.1 0.0 copy-done.5
  44.1 2.4 %fusion.37 = bf16[1536,128]{0,1:T(8,128)(2,1)} fusion(bf16[1,1536,1536]{2,1,0:T(8,128)(2,1)S(1)} %bitcast.120, bf16[1536,256]{0,1:T(8,128)(2,1)S(1)} %fusion.25), kind=kOutput, calls=%fused_computation.30 | convolution fusion | flops 604176384 | bytes 5505024 | tf_op jit(solution)/shard_map/dot_general | solution.py:26
  46.5 2.1 %collective-permute-start = (bf16[1536,128]{0,1:T(8,128)(2,1)}, bf16[1536,128]{0,1:T(8,128)(2,1)S(1)}, u32[]{:S(2)}, u32[]{:S(2)}) collective-permute-start(bf16[1536,128]{0,1:T(8,128)(2,1)} %fusion.37), channel_id=1, source_target_pairs={{0,16},{16,0},{1,17},{17,1},{2,18},{18,2},{3,19},{19,3},{4,20},{20... | collective-permute-start | bytes 1179656 | tf_op jit(solution)/shard_map/ppermute | solution.py:30
  48.5 0.0 slice-start.2
  48.5 3.6 %fusion = bf16[1,1536,1536]{2,1,0:T(8,128)(2,1)} fusion(bf16[1536,256]{0,1:T(8,128)(2,1)S(1)} %fusion.25, bf16[1536,128]{1,0:T(8,128)(2,1)S(1)} %bitcast.136, bf16[1536,128]{1,0:T(8,128)(2,1)S(1)} %bitcast.138), kind=kOutput, calls=%fused_computation.2 | convolution fusion | flops 1211891712 | bytes 6291456 | tf_op jit(solution)/shard_map/dot_general | solution.py:26
  52.1 0.0 slice-start.3
  52.1 5.4 %fusion.1 = bf16[1,1536,1536]{2,1,0:T(8,128)(2,1)} fusion(f32[1536,256]{0,1:T(8,128)} %copy-done.5, bf16[1536,128]{1,0:T(8,128)(2,1)S(1)} %bitcast.134, bf16[1536,128]{1,0:T(8,128)(2,1)S(1)} %bitcast.132), kind=kOutput, calls=%fused_computation.3 | convolution fusion | flops 1215430656 | bytes 7077888 | tf_op jit(solution)/shard_map/dot_general | solution.py:26
  57.5 0.3 collective-permute-done
  57.8 0.0 slice-done.2
  57.8 0.0 slice-done.3
  57.8 1.6 %add_convert_fusion = bf16[1536,128]{0,1:T(8,128)(2,1)S(1)} fusion(bf16[1536,128]{0,1:T(8,128)(2,1)S(1)} %collective-permute-done, bf16[1,1536,1536]{2,1,0:T(8,128)(2,1)S(1)} %bitcast.122, bf16[1536,256]{0,1:T(8,128)(2,1)S(1)} %fusion.25), kind=kOutput, calls=%fused_computation.55 | convolution fusion | flops 604569600 | bytes 5898240 | tf_op jit(solution)/shard_map/dot_general | solution.py:26
  59.5 0.9 copy.14
  60.4 7.9 %all-to-all-start = ((bf16[16,96,128]{2,1,0:T(8,128)(2,1)}), bf16[16,96,128]{2,1,0:T(8,128)(2,1)S(1)}, u32[]{:S(2)}, u32[]{:S(2)}) async-start(bf16[16,96,128]{2,1,0:T(8,128)(2,1)} %bitcast.22), calls=%async_computation | async-start | bytes 786432 | tf_op jit(solution)/shard_map/all_to_all | solution.py:269
  68.3 0.0 collective-permute-done.2
  68.4 0.1 slice_dynamic-update-slice_fusion.3
  68.5 0.1 slice_dynamic-update-slice_fusion.2
  68.7 0.1 slice_dynamic-update-slice_fusion.1
  68.8 0.1 slice_dynamic-update-slice_fusion
  68.9 11.6 %all-to-all-done = bf16[16,96,128]{2,1,0:T(8,128)(2,1)S(1)} async-done(((bf16[16,96,128]{2,1,0:T(8,128)(2,1)}), bf16[16,96,128]{2,1,0:T(8,128)(2,1)S(1)}, u32[]{:S(2)}, u32[]{:S(2)}) %all-to-all-start) | async-done | bytes 393248 | tf_op jit(solution)/shard_map/all_to_all | solution.py:269
  80.5 0.0 copy-done.4
  80.5 1.1 fusion.86
  81.6 26.8 %shard_map.112 = bf16[16,96,512]{2,1,0:T(8,128)(2,1)S(1)} custom-call(bf16[96,512]{1,0:T(8,128)(2,1)S(1)} %get-tuple-element.22.cells), custom_call_target="tpu_custom_call" | custom-call | tf_op jit(solution)/shard_map/pallas_call | solution.py:120
  108.4 0.1 fusion.120
  108.6 0.0 copy-done
  108.6 0.5 convolution_bitcast_fusion
  109.1 0.5 convolution_bitcast_fusion.1
  109.7 0.6 fusion.60
  110.3 0.2 pad_maximum_fusion
  110.5 0.5 fusion.66
  111.0 0.2 collective-permute-start.1
  111.1 1.7 %convolution_add_fusion = f32[480,768]{1,0:T(8,128)} fusion(f32[480,768]{1,0:T(8,128)S(1)} %fusion.60, bf16[768,512]{1,0:T(8,128)(2,1)S(1)} %bitcast.125, bf16[480,1024]{1,0:T(8,128)(2,1)S(1)} %slice_dynamic-update-slice_fusion), kind=kOutput, calls=%fused_computation.44 | convolution fusion | flops 377856000 | bytes 4227072 | tf_op jit(solution)/shard_map/dot_general | solution.py:26
  112.8 3.3 %collective-permute-done.1 = bf16[96,512]{1,0:T(8,128)(2,1)S(1)} collective-permute-done((bf16[96,512]{1,0:T(8,128)(2,1)S(1)}, bf16[96,512]{1,0:T(8,128)(2,1)S(1)}, u32[]{:S(2)}, u32[]{:S(2)}) %collective-permute-start.1) | collective-permute-done | bytes 98336 | tf_op jit(solution)/shard_map/ppermute | solution.py:30
  116.1 0.7 add_convert_fusion.1
  (11 shorter events, 0.1 us)
Async XLA Ops:
  0.6 108.0 %copy-start = (bf16[5,96,768]{2,1,0:T(8,128)(2,1)S(1)}, bf16[5,96,768]{2,1,0:T(8,128)(2,1)}, u32[]{:S(2)}) copy-start(bf16[5,96,768]{2,1,0:T(8,128)(2,1)} %param.11) | copy-start | bytes 2211844
  0.6 67.7 %collective-permute-start.2 = (bf16[96,512]{1,0:T(8,128)(2,1)}, bf16[96,512]{1,0:T(8,128)(2,1)S(1)}, u32[]{:S(2)}, u32[]{:S(2)}) collective-permute-start(bf16[96,512]{1,0:T(8,128)(2,1)} %param.8), channel_id=1, source_target_pairs={{0,16},{16,0},{1,17},{17,1},{2,18},{18,2},{3,19},{19,3},{4,20},{20... | collective-permute-start | bytes 294920 | tf_op jit(solution)/shard_map/ppermute | solution.py:30
  6.2 1.7 %copy-start.1 = (bf16[96,512]{1,0:T(8,128)(2,1)S(1)}, bf16[96,512]{1,0:T(8,128)(2,1)}, u32[]{:S(2)}) copy-start(bf16[96,512]{1,0:T(8,128)(2,1)} %param.8) | copy-start | bytes 294916
  6.2 1.7 %copy-start.3 = (bf16[96,512]{1,0:T(8,128)(2,1)S(1)}, bf16[96,512]{1,0:T(8,128)(2,1)}, u32[]{:S(2)}) copy-start(bf16[96,512]{1,0:T(8,128)(2,1)} %param.9) | copy-start | bytes 294916
  8.0 1.3 %copy-start.2 = (bf16[96,512]{1,0:T(8,128)(2,1)S(1)}, bf16[96,512]{1,0:T(8,128)(2,1)}, u32[]{:S(2)}) copy-start(bf16[96,512]{1,0:T(8,128)(2,1)} %param.10) | copy-start | bytes 294916
  9.3 30.5 %slice-start = ((s8[4718592]{0:T(1024)(128)(4,1)}), s8[4194304]{0:T(1024)(128)(4,1)S(1)}, s32[]{:S(2)}) async-start(s8[4718592]{0:T(1024)(128)(4,1)} %bitcast.119), calls=%async_computation.1 | async-start | bytes 8388608
  10.7 29.1 %slice-start.1 = ((s8[4718592]{0:T(1024)(128)(4,1)}), s8[524288]{0:T(1024)(128)(4,1)S(1)}, s32[]{:S(2)}) async-start(s8[4718592]{0:T(1024)(128)(4,1)} %bitcast.119), calls=%async_computation.2 | async-start | bytes 1048576
  39.7 2.2 %slice-start.4 = ((s8[4718592]{0:T(1024)(128)(4,1)}), s8[4194304]{0:T(1024)(128)(4,1)S(1)}, s32[]{:S(2)}) async-start(s8[4718592]{0:T(1024)(128)(4,1)} %bitcast.154), calls=%async_computation.5 | async-start | bytes 8388608
  39.8 2.2 %slice-start.5 = ((s8[4718592]{0:T(1024)(128)(4,1)}), s8[524288]{0:T(1024)(128)(4,1)S(1)}, s32[]{:S(2)}) async-start(s8[4718592]{0:T(1024)(128)(4,1)} %bitcast.154), calls=%async_computation.6 | async-start | bytes 1048576
  41.2 2.8 %copy-start.5 = (f32[1536,256]{0,1:T(8,128)}, f32[1536,256]{0,1:T(8,128)S(1)}, u32[]{:S(2)}) copy-start(f32[1536,256]{0,1:T(8,128)S(1)} %fusion.22) | copy-start | bytes 4718596
  46.5 11.4 %collective-permute-start = (bf16[1536,128]{0,1:T(8,128)(2,1)}, bf16[1536,128]{0,1:T(8,128)(2,1)S(1)}, u32[]{:S(2)}, u32[]{:S(2)}) collective-permute-start(bf16[1536,128]{0,1:T(8,128)(2,1)} %fusion.37), channel_id=1, source_target_pairs={{0,16},{16,0},{1,17},{17,1},{2,18},{18,2},{3,19},{19,3},{4,20},{20... | collective-permute-start | bytes 1179656 | tf_op jit(solution)/shard_map/ppermute | solution.py:30
  48.5 9.3 %slice-start.2 = ((s8[4718592]{0:T(1024)(128)(4,1)}), s8[524288]{0:T(1024)(128)(4,1)S(1)}, s32[]{:S(2)}) async-start(s8[4718592]{0:T(1024)(128)(4,1)} %bitcast.121), calls=%async_computation.3 | async-start | bytes 1048576
  52.1 5.7 %slice-start.3 = ((s8[4718592]{0:T(1024)(128)(4,1)}), s8[4194304]{0:T(1024)(128)(4,1)S(1)}, s32[]{:S(2)}) async-start(s8[4718592]{0:T(1024)(128)(4,1)} %bitcast.121), calls=%async_computation.4 | async-start | bytes 8388608
  60.4 20.1 %copy-start.4 = (bf16[96,512]{1,0:T(8,128)(2,1)S(1)}, bf16[96,512]{1,0:T(8,128)(2,1)}, u32[]{:S(2)}) copy-start(bf16[96,512]{1,0:T(8,128)(2,1)} %param.9) | copy-start | bytes 294916
  60.4 20.1 %all-to-all-start = ((bf16[16,96,128]{2,1,0:T(8,128)(2,1)}), bf16[16,96,128]{2,1,0:T(8,128)(2,1)S(1)}, u32[]{:S(2)}, u32[]{:S(2)}) async-start(bf16[16,96,128]{2,1,0:T(8,128)(2,1)} %bitcast.22), calls=%async_computation | async-start | bytes 786432 | tf_op jit(solution)/shard_map/all_to_all | solution.py:269
  111.0 5.1 %collective-permute-start.1 = (bf16[96,512]{1,0:T(8,128)(2,1)S(1)}, bf16[96,512]{1,0:T(8,128)(2,1)S(1)}, u32[]{:S(2)}, u32[]{:S(2)}) collective-permute-start(bf16[96,512]{1,0:T(8,128)(2,1)S(1)} %select_convert_fusion), channel_id=1, source_target_pairs={{0,16},{16,0},{1,17},{17,1},{2,18},{18,2},{3,19},{19,3},{4,20},{20... | collective-permute-start | bytes 294920 | tf_op jit(solution)/shard_map/ppermute | solution.py:30

commit v4 on v3

--- a/solution.py
+++ b/solution.py
@@ -194,6 +194,65 @@
     )(cells)
 
 
+def return_kernel(theirs, mine, out, got, summed, y_sent, y_got, a_sent, a_got):
+    c, e = lax.axis_index("ctx"), lax.axis_index("exp")
+    size = mine.shape[0]
+    other = (1 - c, e)
+
+    def to(d):
+        return lax.rem(e + d, size)
+
+    def source(d):
+        return lax.rem(e + size - d, size)
+
+    barrier = pltpu.get_barrier_semaphore()
+    greet(barrier, [(c, to(d)) for d in range(1, size)] + [other])
+    pl.semaphore_wait(barrier, size)
+
+    def crossing(d):
+        return remote(theirs.at[to(d)], got.at[to(d)], y_sent.at[d], y_got.at[d], other)
+
+    def sending(d):
+        return remote(summed.at[to(d)], out.at[e], a_sent.at[d], a_got.at[d], (c, to(d)))
+
+    def arriving(d):
+        slot = source(d)
+        return remote(summed.at[slot], out.at[slot], a_sent.at[d], a_got.at[d], (c, slot))
+
+    order = [*range(1, size), 0]
+    for d in order:
+        crossing(d).start()
+    for d in order:
+        crossing(d).wait_recv()
+        total = (mine[to(d)] + got[to(d)].astype(F32)).astype(BF16)
+        if d:
+            summed[to(d)] = total
+            sending(d).start()
+        else:
+            out[e] = total
+    for d in range(1, size):
+        arriving(d).wait_recv()
+        sending(d).wait_send()
+    for d in order:
+        crossing(d).wait_send()
+
+
+def returned(theirs, mine):
+    size = mine.shape[0]
+    dma = pltpu.SemaphoreType.DMA
+    return pl.pallas_call(
+        return_kernel,
+        out_shape=jax.ShapeDtypeStruct(theirs.shape, theirs.dtype),
+        in_specs=[pl.BlockSpec(memory_space=pltpu.VMEM)] * 2,
+        out_specs=pl.BlockSpec(memory_space=pltpu.VMEM),
+        scratch_shapes=[pltpu.VMEM(theirs.shape, theirs.dtype)] * 2
+        + [dma((size,)), dma((size,)), dma((size,)), dma((size,))],
+        compiler_params=pltpu.CompilerParams(
+            collective_id=2, has_side_effects=True, vmem_limit_bytes=24 * 2**20
+        ),
+    )(theirs, mine)
+
+
 def local(inputs, pre_act, grad_out, conv_weight, expert_ids, gate_values, expert_in, expert_out):
     channels, bins = inputs.shape
     experts = lax.axis_size("exp")
@@ -258,7 +317,8 @@
     if pair:
         theirs = product(first, grad_pre[:, capacity:], ((1,), (0,))).astype(BF16)
         mine = product(first, grad_pre[:, :capacity], ((1,), (0,)))
-        back = (mine + swapped(theirs).astype(F32)).astype(BF16)
+        if experts != 16:
+            back = (mine + swapped(theirs).astype(F32)).astype(BF16)
     else:
         part = product(first, grad_pre, ((1,), (0,)))
         back = lax.psum_scatter(part, "ctx", scatter_dimension=1, tiled=True).astype(BF16)
@@ -266,9 +326,13 @@
     grad_second = product(squashed, rows_grad, ((1,), (1,))).astype(BF16)
     grad_first = product(rows_in, grad_pre, ((1,), (1,))).astype(BF16)
 
-    back = lax.all_to_all(
-        back.reshape(experts, channels, capacity), "exp", split_axis=0, concat_axis=0, tiled=True
-    )
+    shape = (experts, channels, capacity)
+    if pair and experts == 16:
+        back = returned(theirs.reshape(shape), mine.reshape(shape))
+    else:
+        back = lax.all_to_all(
+            back.reshape(shape), "exp", split_axis=0, concat_axis=0, tiled=True
+        )
     back = back.transpose(1, 0, 2).reshape(channels, experts * capacity)
     grad_total = grad_float + product(back, pick_any, ((1,), (0,)))
     grad_pre_conv = (grad_total * gelu_slope(pre_float)).astype(BF16)

time: 117 us -> 118 us (level)
  Pallas kernels: 55.6 us -> 79.2 us
  waiting for transfers between devices: 15.2 us -> 0.01 us
  starting transfers between devices: 13.2 us -> 3.1 us
    pallas_call x0 -> x1, Pallas kernels: none -> 21 us  [returned(): pl.pallas_call(return_kernel, out_shape=jax.ShapeDtypeStruct(theirs.shape...]
    all_to_all x1 -> x0, waiting for transfers between devices: 11.6 us -> none  [local(): lax.all_to_all(back.reshape(experts, channels, capacity), 'exp', split_ax...]
    all_to_all x1 -> x0, starting transfers between devices: 7.91 us -> none  [local(): lax.all_to_all(back.reshape(experts, channels, capacity), 'exp', split_ax...]
    ppermute x3 -> x2, waiting for transfers between devices: 3.6 us -> 0.01 us  [swapped(): return lax.ppermute(block, 'ctx', [(0, 1), (1, 0)])]
    pallas_call x1, Pallas kernels: 26.8 us -> 29.5 us  [gathered(): pl.pallas_call(gather_kernel, out_shape=jax.ShapeDtypeStruct((size,) + ce...]
    ppermute x3 -> x2, starting transfers between devices: 5.24 us -> 3.1 us  [swapped(): return lax.ppermute(block, 'ctx', [(0, 1), (1, 0)])]
  transfers between devices with their start and end apart: 4 -> 2, of which waited for: 3 -> 0; matrix products, arithmetic and copies ran while one was open for 23% -> 27% of each run, Pallas kernels for 25% -> 67%
where the time goes in v4:
time: 118 us
  Pallas kernels  79.2 us (67%)
  matrix products  24.7 us (21%)
  other arithmetic  4.89 us (4%)
  local copies, waits for them, and re-layouts  4.75 us (4%)
  starting transfers between devices  3.1 us (3%)
    pallas_call x1, Pallas kernels, gathered(): pl.pallas_call(gather_kernel, out_shape=jax.ShapeDtypeStruct((size,) + ce...  29.5 us
    pallas_call x1, Pallas kernels, spread_rows(): pl.pallas_call(spread_kernel, out_shape=jax.ShapeDtypeStruct((2,) + cells...  28.8 us
    dot_general x14, matrix products, product(): lax.dot_general(left, right, (dims, ((), ())), preferred_element_type=F32)  24.7 us
    pallas_call x1, Pallas kernels, returned(): pl.pallas_call(return_kernel, out_shape=jax.ShapeDtypeStruct(theirs.shape...  21 us
    ppermute x2, starting transfers between devices, swapped(): return lax.ppermute(block, 'ctx', [(0, 1), (1, 0)])  3.1 us
  transfers between devices with their start and end apart: 2, of which 0 were waited for; matrix products, arithmetic and copies ran while one was open for 27% of the time, Pallas kernels for 67%

profile of v4, /device:TPU:0, one launch (start us, length us, event | category | flops | bytes accessed | tf_op | source)
XLA Modules:
  0.0 117.8 jit_solution(11855397943497038632)
XLA Ops:
  0.6 0.0 copy-start
  0.6 3.0 %collective-permute-start.1 = (bf16[96,512]{1,0:T(8,128)(2,1)}, bf16[96,512]{1,0:T(8,128)(2,1)}, u32[]{:S(2)}, u32[]{:S(2)}) collective-permute-start(bf16[96,512]{1,0:T(8,128)(2,1)} %param.8), channel_id=1, source_target_pairs={{0,16},{16,0},{1,17},{17,1},{2,18},{18,2},{3,19},{19,3},{4,20},{20... | collective-permute-start | bytes 294920 | tf_op jit(solution)/shard_map/ppermute | solution.py:30
  3.7 0.8 fusion.119
  4.4 0.2 select_reduce_fusion.1
  4.7 0.8 fusion.118
  5.4 0.8 multiply_add_fusion.2
  6.2 0.0 copy-start.9
  6.2 0.0 copy-start.11
  6.2 1.7 %fusion.14 = (bf16[2048,512]{1,0:T(8,128)(2,1)S(1)}, bf16[2048,512]{1,0:T(8,128)(2,1)S(1)}) fusion(s32[512]{0:T(512)S(1)} %bitcast.138, s32[512]{0:T(512)S(1)} %bitcast.141), kind=kLoop, calls=%fused_computation.18 | loop fusion | flops 4194304 | bytes 4198400 | tf_op jit(solution)/shard_map/convert_element_type | solution.py:277
  7.9 0.0 copy-done.9
  8.0 0.0 copy-done.11
  8.0 0.0 copy-start.8
  8.0 1.2 %fusion.45 = bf16[12,16,8,128]{3,2,1,0:T(8,128)(2,1)S(1)} fusion(s32[512]{0:T(512)S(1)} %bitcast.142, s32[512]{0:T(512)S(1)} %bitcast.139, bf16[96,512]{1,0:T(8,128)(2,1)S(1)} %copy-done.11, bf16[96,512]{1,0:T(8,128)(2,1)S(1)} %copy-done.9), kind=kOutput, calls=%fused_computation.47 | convolution fusion | flops 210501632 | bytes 593920 | tf_op jit(solution)/shard_map/dot_general | solution.py:26
  9.2 0.1 copy.31
  9.3 0.0 copy-done.8
  9.3 0.0 slice-start
  9.3 1.4 %fusion.46 = bf16[12,16,8,128]{3,2,1,0:T(8,128)(2,1)S(1)} fusion(bf16[2048,512]{1,0:T(8,128)(2,1)S(1)} %get-tuple-element.25, bf16[2048,512]{1,0:T(8,128)(2,1)S(1)} %get-tuple-element.24, bf16[96,512]{1,0:T(8,128)(2,1)S(1)} %get-tuple-element.15, bf16[96,512]{1,0:T(8,128)(2,1)S(1)} %get-tuple-element.14), kind=kOutput, calls=%fused_computation.48 | convolution fusion | flops 411631616 | bytes 4784128 | tf_op jit(solution)/shard_map/dot_general | solution.py:26
  10.7 0.0 slice-start.1
  10.7 0.1 copy.30
  10.8 0.1 pad_maximum_fusion.1.cells
  10.9 28.8 %shard_map.111 = bf16[2,16,192,128]{3,2,1,0:T(8,128)(2,1)S(1)} custom-call(bf16[16,192,128]{2,1,0:T(8,128)(2,1)S(1)} %pad_maximum_fusion.1.cells), custom_call_target="tpu_custom_call" | custom-call | tf_op jit(solution)/shard_map/pallas_call | solution.py:185
  39.7 0.0 slice-start.2
  39.7 0.1 fusion.117
  39.8 0.0 copy-start.1
  39.8 0.0 copy-start.3
  39.9 0.0 copy-start.5
  39.9 0.0 copy-start.6
  39.9 0.0 slice-done
  39.9 0.0 slice-done.1
  39.9 0.0 slice-start.3
  39.9 1.4 %fusion.22 = f32[1536,256]{0,1:T(8,128)S(1)} fusion(bf16[1,1536,1536]{2,1,0:T(8,128)(2,1)S(1)} %bitcast.119, bf16[1536,128]{1,0:T(8,128)(2,1)S(1)} %bitcast.128, bf16[1536,128]{1,0:T(8,128)(2,1)S(1)} %bitcast.130), kind=kOutput, calls=%fused_computation.22 | convolution fusion | flops 1209532416 | bytes 7077888 | tf_op jit(solution)/shard_map/dot_general | solution.py:26
  41.3 0.0 copy-done.1
  41.3 0.0 copy-done.3
  41.4 0.0 copy-start.12
  41.4 1.4 %slice-done.2 = s8[4194304]{0:T(1024)(128)(4,1)S(1)} async-done(((s8[4718592]{0:T(1024)(128)(4,1)}), s8[4194304]{0:T(1024)(128)(4,1)S(1)}, s32[]{:S(2)}) %slice-start.2) | async-done | bytes 4194328
  42.8 0.4 slice-done.3
  43.1 2.1 %fusion.25 = bf16[1536,256]{0,1:T(8,128)(2,1)S(1)} fusion(bf16[1,1536,1536]{2,1,0:T(8,128)(2,1)S(1)} %bitcast.152, f32[1536,256]{0,1:T(8,128)S(1)} %fusion.22, bf16[1536,128]{1,0:T(8,128)(2,1)S(1)} %bitcast.134, bf16[1536,128]{1,0:T(8,128)(2,1)S(1)} %bitcast.132), kind=kOutput, calls=%fused_computation.23 | convolution fusion | flops 1217003520 | bytes 7864320 | tf_op jit(solution)/shard_map/dot_general | solution.py:26
  45.2 1.6 %fusion.37 = bf16[1536,128]{0,1:T(8,128)(2,1)S(1)} fusion(bf16[1,1536,1536]{2,1,0:T(8,128)(2,1)S(1)} %bitcast.119, bf16[1536,256]{0,1:T(8,128)(2,1)S(1)} %fusion.25), kind=kOutput, calls=%fused_computation.30 | convolution fusion | flops 604176384 | bytes 5505024 | tf_op jit(solution)/shard_map/dot_general | solution.py:26
  46.9 1.6 %fusion.28 = f32[1536,128]{0,1:T(8,128)S(1)} fusion(bf16[1,1536,1536]{2,1,0:T(8,128)(2,1)S(1)} %bitcast.119, bf16[1536,256]{0,1:T(8,128)(2,1)S(1)} %fusion.25), kind=kOutput, calls=%fused_computation.24 | convolution fusion | flops 603979776 | bytes 5898240 | tf_op jit(solution)/shard_map/dot_general | solution.py:26
  48.5 0.2 copy.16
  48.7 0.3 copy.17
  49.0 21.0 %shard_map.112 = bf16[16,96,128]{2,1,0:T(8,128)(2,1)S(1)} custom-call(bf16[16,96,128]{2,1,0:T(8,128)(2,1)S(1)} %bitcast.117, f32[16,96,128]{2,1,0:T(8,128)S(1)} %bitcast.116), custom_call_target="tpu_custom_call" | custom-call | tf_op jit(solution)/shard_map/pallas_call | solution.py:243
  70.0 2.7 %fusion.82 = (bf16[96,512]{1,0:T(8,128)(2,1)S(1)}, f32[96,512]{1,0:T(8,128)}) fusion(bf16[96,512]{1,0:T(8,128)(2,1)} %param.9, s32[512]{0:T(512)S(1)} %bitcast.143, s32[512]{0:T(512)S(1)} %bitcast.140, bf16[96,512]{1,0:T(8,128)(2,1)} %param.10, bf16[16,96,128]{2,1,0:T(8,128)(2,1)S(1)} %shard_map.112), kind=kOutput, calls=%fused_computation.94 | convolution fusion | flops 210796544 | bytes 888832 | tf_op jit(solution)/shard_map/dot_general | solution.py:26
  72.6 29.5 %shard_map.113 = bf16[16,96,512]{2,1,0:T(8,128)(2,1)S(1)} custom-call(bf16[96,512]{1,0:T(8,128)(2,1)S(1)} %get-tuple-element.22.cells), custom_call_target="tpu_custom_call" | custom-call | tf_op jit(solution)/shard_map/pallas_call | solution.py:120
  102.2 0.1 fusion.116
  102.3 0.5 convolution_bitcast_fusion
  102.9 0.5 convolution_bitcast_fusion.1
  103.4 0.2 pad_maximum_fusion
  103.6 0.5 fusion.66
  104.1 0.0 copy-start.2
  104.1 0.0 copy-start.4
  104.1 0.1 collective-permute-start
  104.2 5.5 %fusion.1 = bf16[1,1536,1536]{2,1,0:T(8,128)(2,1)} fusion(f32[1536,256]{0,1:T(8,128)} %copy-done.12, bf16[1536,128]{1,0:T(8,128)(2,1)} %bitcast.135, bf16[1536,128]{1,0:T(8,128)(2,1)} %bitcast.133), kind=kOutput, calls=%fused_computation.3 | convolution fusion | flops 1215430656 | bytes 7077888 | tf_op jit(solution)/shard_map/dot_general | solution.py:26
  109.7 3.6 %fusion = bf16[1,1536,1536]{2,1,0:T(8,128)(2,1)} fusion(bf16[1536,256]{0,1:T(8,128)(2,1)S(1)} %fusion.25, bf16[1536,128]{1,0:T(8,128)(2,1)S(1)} %bitcast.129, bf16[1536,128]{1,0:T(8,128)(2,1)S(1)} %bitcast.131), kind=kOutput, calls=%fused_computation.2 | convolution fusion | flops 1211891712 | bytes 6291456 | tf_op jit(solution)/shard_map/dot_general | solution.py:26
  113.3 0.0 collective-permute-done.1
  113.3 0.9 broadcast_select_fusion.1
  114.2 0.1 slice_dynamic-update-slice_fusion.3
  114.3 0.1 slice_dynamic-update-slice_fusion.2
  114.5 0.1 slice_dynamic-update-slice_fusion.1
  114.6 0.1 slice_dynamic-update-slice_fusion
  114.7 0.6 fusion.60
  115.3 1.7 %convolution_add_fusion = f32[480,768]{1,0:T(8,128)} fusion(f32[480,768]{1,0:T(8,128)S(1)} %fusion.60, bf16[768,512]{1,0:T(8,128)(2,1)S(1)} %bitcast.122, bf16[480,1024]{1,0:T(8,128)(2,1)S(1)} %slice_dynamic-update-slice_fusion), kind=kOutput, calls=%fused_computation.44 | convolution fusion | flops 377856000 | bytes 4227072 | tf_op jit(solution)/shard_map/dot_general | solution.py:26
  117.0 0.0 collective-permute-done
  117.1 0.7 add_convert_fusion
  (18 shorter events, 0.1 us)
Async XLA Ops:
  0.6 101.7 %copy-start = (bf16[5,96,768]{2,1,0:T(8,128)(2,1)S(1)}, bf16[5,96,768]{2,1,0:T(8,128)(2,1)}, u32[]{:S(2)}) copy-start(bf16[5,96,768]{2,1,0:T(8,128)(2,1)} %param.11) | copy-start | bytes 2211844
  0.6 112.6 %collective-permute-start.1 = (bf16[96,512]{1,0:T(8,128)(2,1)}, bf16[96,512]{1,0:T(8,128)(2,1)}, u32[]{:S(2)}, u32[]{:S(2)}) collective-permute-start(bf16[96,512]{1,0:T(8,128)(2,1)} %param.8), channel_id=1, source_target_pairs={{0,16},{16,0},{1,17},{17,1},{2,18},{18,2},{3,19},{19,3},{4,20},{20... | collective-permute-start | bytes 294920 | tf_op jit(solution)/shard_map/ppermute | solution.py:30
  6.2 1.7 %copy-start.9 = (bf16[96,512]{1,0:T(8,128)(2,1)S(1)}, bf16[96,512]{1,0:T(8,128)(2,1)}, u32[]{:S(2)}) copy-start(bf16[96,512]{1,0:T(8,128)(2,1)} %param.8) | copy-start | bytes 294916
  6.2 1.7 %copy-start.11 = (bf16[96,512]{1,0:T(8,128)(2,1)S(1)}, bf16[96,512]{1,0:T(8,128)(2,1)}, u32[]{:S(2)}) copy-start(bf16[96,512]{1,0:T(8,128)(2,1)} %param.9) | copy-start | bytes 294916
  8.0 1.3 %copy-start.8 = (bf16[96,512]{1,0:T(8,128)(2,1)S(1)}, bf16[96,512]{1,0:T(8,128)(2,1)}, u32[]{:S(2)}) copy-start(bf16[96,512]{1,0:T(8,128)(2,1)} %param.10) | copy-start | bytes 294916
  9.3 30.6 %slice-start = ((s8[4718592]{0:T(1024)(128)(4,1)}), s8[4194304]{0:T(1024)(128)(4,1)S(1)}, s32[]{:S(2)}) async-start(s8[4718592]{0:T(1024)(128)(4,1)} %bitcast.118), calls=%async_computation | async-start | bytes 8388608
  10.7 29.2 %slice-start.1 = ((s8[4718592]{0:T(1024)(128)(4,1)}), s8[524288]{0:T(1024)(128)(4,1)S(1)}, s32[]{:S(2)}) async-start(s8[4718592]{0:T(1024)(128)(4,1)} %bitcast.118), calls=%async_computation.1 | async-start | bytes 1048576
  39.7 3.1 %slice-start.2 = ((s8[4718592]{0:T(1024)(128)(4,1)}), s8[4194304]{0:T(1024)(128)(4,1)S(1)}, s32[]{:S(2)}) async-start(s8[4718592]{0:T(1024)(128)(4,1)} %bitcast.151), calls=%async_computation.2 | async-start | bytes 8388608
  39.8 1.5 %copy-start.1 = (bf16[1,16,96,128]{3,2,1,0:T(8,128)(2,1)}, bf16[1,16,96,128]{3,2,1,0:T(8,128)(2,1)S(1)}, u32[]{:S(2)}) copy-start(bf16[1,16,96,128]{3,2,1,0:T(8,128)(2,1)S(1)} %get-tuple-element.9) | copy-start | bytes 1179652
  39.8 1.5 %copy-start.3 = (bf16[1,16,96,128]{3,2,1,0:T(8,128)(2,1)}, bf16[1,16,96,128]{3,2,1,0:T(8,128)(2,1)S(1)}, u32[]{:S(2)}) copy-start(bf16[1,16,96,128]{3,2,1,0:T(8,128)(2,1)S(1)} %get-tuple-element.10) | copy-start | bytes 1179652
  39.9 1.5 %copy-start.5 = (bf16[1,16,96,128]{3,2,1,0:T(8,128)(2,1)}, bf16[1,16,96,128]{3,2,1,0:T(8,128)(2,1)S(1)}, u32[]{:S(2)}) copy-start(bf16[1,16,96,128]{3,2,1,0:T(8,128)(2,1)S(1)} %get-tuple-element.8) | copy-start | bytes 1179652
  39.9 5.3 %copy-start.6 = (bf16[1,16,96,128]{3,2,1,0:T(8,128)(2,1)}, bf16[1,16,96,128]{3,2,1,0:T(8,128)(2,1)S(1)}, u32[]{:S(2)}) copy-start(bf16[1,16,96,128]{3,2,1,0:T(8,128)(2,1)S(1)} %get-tuple-element.11) | copy-start | bytes 1179652
  39.9 3.2 %slice-start.3 = ((s8[4718592]{0:T(1024)(128)(4,1)}), s8[524288]{0:T(1024)(128)(4,1)S(1)}, s32[]{:S(2)}) async-start(s8[4718592]{0:T(1024)(128)(4,1)} %bitcast.151), calls=%async_computation.3 | async-start | bytes 1048576
  41.4 3.9 %copy-start.12 = (f32[1536,256]{0,1:T(8,128)}, f32[1536,256]{0,1:T(8,128)S(1)}, u32[]{:S(2)}) copy-start(f32[1536,256]{0,1:T(8,128)S(1)} %fusion.22) | copy-start | bytes 4718596
  104.1 5.6 %copy-start.2 = (bf16[1,16,96,128]{3,2,1,0:T(8,128)(2,1)S(1)}, bf16[1,16,96,128]{3,2,1,0:T(8,128)(2,1)}, u32[]{:S(2)}) copy-start(bf16[1,16,96,128]{3,2,1,0:T(8,128)(2,1)} %copy-done.1) | copy-start | bytes 1179652
  104.1 5.6 %copy-start.4 = (bf16[1,16,96,128]{3,2,1,0:T(8,128)(2,1)S(1)}, bf16[1,16,96,128]{3,2,1,0:T(8,128)(2,1)}, u32[]{:S(2)}) copy-start(bf16[1,16,96,128]{3,2,1,0:T(8,128)(2,1)} %copy-done.3) | copy-start | bytes 1179652
  104.1 12.9 %collective-permute-start = (bf16[96,512]{1,0:T(8,128)(2,1)S(1)}, bf16[96,512]{1,0:T(8,128)(2,1)S(1)}, u32[]{:S(2)}, u32[]{:S(2)}) collective-permute-start(bf16[96,512]{1,0:T(8,128)(2,1)S(1)} %select_convert_fusion), channel_id=1, source_target_pairs={{0,16},{16,0},{1,17},{17,1},{2,18},{18,2},{3,19},{19,3},{4,20},{20... | collective-permute-start | bytes 294920 | tf_op jit(solution)/shard_map/ppermute | solution.py:30
  109.7 3.6 %copy-start.10 = (bf16[96,512]{1,0:T(8,128)(2,1)S(1)}, bf16[96,512]{1,0:T(8,128)(2,1)}, u32[]{:S(2)}) copy-start(bf16[96,512]{1,0:T(8,128)(2,1)} %param.8) | copy-start | bytes 294916
  115.3 1.7 %copy-start.7 = (f32[96,512]{1,0:T(8,128)S(1)}, f32[96,512]{1,0:T(8,128)}, u32[]{:S(2)}) copy-start(f32[96,512]{1,0:T(8,128)} %get-tuple-element.23) | copy-start | bytes 589828

commit v5 on v3

--- a/solution.py
+++ b/solution.py
@@ -264,6 +264,7 @@
         back = lax.psum_scatter(part, "ctx", scatter_dimension=1, tiled=True).astype(BF16)
     squashed = gelu_value(hidden).astype(BF16)
     grad_second = product(squashed, rows_grad, ((1,), (1,))).astype(BF16)
+    grad_pre, back = lax.optimization_barrier((grad_pre, back))
     grad_first = product(rows_in, grad_pre, ((1,), (1,))).astype(BF16)
 
     back = lax.all_to_all(

time: 117 us -> 120 us (1.026)
  matrix products: 23.7 us -> 25.7 us
    ppermute x3, waiting for transfers between devices: 3.6 us -> 8.45 us  [swapped(): return lax.ppermute(block, 'ctx', [(0, 1), (1, 0)])]
    all_to_all x1, waiting for transfers between devices: 11.6 us -> 7.14 us  [local(): lax.all_to_all(back.reshape(experts, channels, capacity), 'exp', split_ax...]
    dot_general x14, matrix products: 23.7 us -> 25.7 us  [product(): lax.dot_general(left, right, (dims, ((), ())), preferred_element_type=F32)]
  transfers between devices with their start and end apart: 4 -> 4, of which waited for: 3 -> 3; matrix products, arithmetic and copies ran while one was open for 23% -> 19% of each run, Pallas kernels for 25% -> 24%
where the time goes in v5:
time: 120 us; the launch traced here: 119 us
  Pallas kernels  55.6 us (46%)
  matrix products  25.7 us (21%)
  waiting for transfers between devices  15.6 us (13%)
  starting transfers between devices  13.1 us (11%)
  local copies, waits for them, and re-layouts  4.19 us (3%)
  other arithmetic  4 us (3%)
    pallas_call x1, Pallas kernels, spread_rows(): pl.pallas_call(spread_kernel, out_shape=jax.ShapeDtypeStruct((2,) + cells...  28.8 us
    pallas_call x1, Pallas kernels, gathered(): pl.pallas_call(gather_kernel, out_shape=jax.ShapeDtypeStruct((size,) + ce...  26.8 us
    dot_general x14, matrix products, product(): lax.dot_general(left, right, (dims, ((), ())), preferred_element_type=F32)  25.7 us
    ppermute x3, waiting for transfers between devices, swapped(): return lax.ppermute(block, 'ctx', [(0, 1), (1, 0)])  8.45 us
    all_to_all x1, starting transfers between devices, local(): lax.all_to_all(back.reshape(experts, channels, capacity), 'exp', split_ax...  7.83 us
    all_to_all x1, waiting for transfers between devices, local(): lax.all_to_all(back.reshape(experts, channels, capacity), 'exp', split_ax...  7.14 us
    ppermute x3, starting transfers between devices, swapped(): return lax.ppermute(block, 'ctx', [(0, 1), (1, 0)])  5.31 us
  transfers between devices with their start and end apart: 4, of which 3 were waited for; matrix products, arithmetic and copies ran while one was open for 19% of the time, Pallas kernels for 24%

profile of v5, /device:TPU:0, one launch (start us, length us, event | category | flops | bytes accessed | tf_op | source)
XLA Modules:
  0.0 119.2 jit_solution(4112122971161060109)
XLA Ops:
  0.6 0.0 copy-start
  0.6 3.0 %collective-permute-start.2 = (bf16[96,512]{1,0:T(8,128)(2,1)}, bf16[96,512]{1,0:T(8,128)(2,1)S(1)}, u32[]{:S(2)}, u32[]{:S(2)}) collective-permute-start(bf16[96,512]{1,0:T(8,128)(2,1)} %param.8), channel_id=1, source_target_pairs={{0,16},{16,0},{1,17},{17,1},{2,18},{18,2},{3,19},{19,3},{4,20},{20... | collective-permute-start | bytes 294920 | tf_op jit(solution)/shard_map/ppermute | solution.py:30
  3.7 0.8 fusion.123
  4.4 0.2 select_reduce_fusion.1
  4.7 0.8 fusion.122
  5.4 0.8 multiply_add_fusion.2
  6.2 0.0 copy-start.2
  6.2 0.0 copy-start.4
  6.2 1.7 %fusion.14 = (bf16[2048,512]{1,0:T(8,128)(2,1)S(1)}, bf16[2048,512]{1,0:T(8,128)(2,1)S(1)}) fusion(s32[512]{0:T(512)S(1)} %bitcast.139, s32[512]{0:T(512)S(1)} %bitcast.142), kind=kLoop, calls=%fused_computation.18 | loop fusion | flops 4194304 | bytes 4198400 | tf_op jit(solution)/shard_map/convert_element_type | solution.py:218
  7.9 0.0 copy-done.2
  8.0 0.0 copy-done.4
  8.0 0.0 copy-start.3
  8.0 1.2 %fusion.45 = bf16[12,16,8,128]{3,2,1,0:T(8,128)(2,1)S(1)} fusion(s32[512]{0:T(512)S(1)} %bitcast.143, s32[512]{0:T(512)S(1)} %bitcast.140, bf16[96,512]{1,0:T(8,128)(2,1)S(1)} %copy-done.4, bf16[96,512]{1,0:T(8,128)(2,1)S(1)} %copy-done.2), kind=kOutput, calls=%fused_computation.47 | convolution fusion | flops 210501632 | bytes 593920 | tf_op jit(solution)/shard_map/dot_general | solution.py:26
  9.2 0.1 copy.28
  9.3 0.0 copy-done.3
  9.3 0.0 slice-start
  9.3 1.4 %fusion.46 = bf16[12,16,8,128]{3,2,1,0:T(8,128)(2,1)S(1)} fusion(bf16[2048,512]{1,0:T(8,128)(2,1)S(1)} %get-tuple-element.29, bf16[2048,512]{1,0:T(8,128)(2,1)S(1)} %get-tuple-element.28, bf16[96,512]{1,0:T(8,128)(2,1)S(1)} %get-tuple-element.19, bf16[96,512]{1,0:T(8,128)(2,1)S(1)} %get-tuple-element.18), kind=kOutput, calls=%fused_computation.48 | convolution fusion | flops 411631616 | bytes 4784128 | tf_op jit(solution)/shard_map/dot_general | solution.py:26
  10.7 0.0 slice-start.1
  10.7 0.1 copy.27
  10.8 0.1 pad_maximum_fusion.1.cells
  10.9 28.8 %shard_map.111 = bf16[2,16,192,128]{3,2,1,0:T(8,128)(2,1)S(1)} custom-call(bf16[16,192,128]{2,1,0:T(8,128)(2,1)S(1)} %pad_maximum_fusion.1.cells), custom_call_target="tpu_custom_call" | custom-call | tf_op jit(solution)/shard_map/pallas_call | solution.py:185
  39.7 0.0 slice-start.2
  39.7 0.1 fusion.121
  39.8 0.0 copy-start.1
  39.8 0.0 slice-done
  39.8 0.0 slice-done.1
  39.8 0.0 slice-start.3
  39.9 1.4 %fusion.22 = f32[1536,256]{0,1:T(8,128)S(1)} fusion(bf16[1,1536,1536]{2,1,0:T(8,128)(2,1)S(1)} %bitcast.120, bf16[1536,128]{1,0:T(8,128)(2,1)S(1)} %bitcast.129, bf16[1536,128]{1,0:T(8,128)(2,1)S(1)} %bitcast.131), kind=kOutput, calls=%fused_computation.22 | convolution fusion | flops 1209532416 | bytes 7077888 | tf_op jit(solution)/shard_map/dot_general | solution.py:26
  41.3 0.0 copy-done.1
  41.3 0.7 slice-done.2
  42.0 0.1 slice-done.3
  42.1 2.0 %fusion.25 = bf16[1536,256]{0,1:T(8,128)(2,1)S(1)} fusion(bf16[1,1536,1536]{2,1,0:T(8,128)(2,1)S(1)} %bitcast.153, f32[1536,256]{0,1:T(8,128)S(1)} %fusion.22, bf16[1536,128]{1,0:T(8,128)(2,1)S(1)} %bitcast.135, bf16[1536,128]{1,0:T(8,128)(2,1)S(1)} %bitcast.133), kind=kOutput, calls=%fused_computation.23 | convolution fusion | flops 1217003520 | bytes 7864320 | tf_op jit(solution)/shard_map/dot_general | solution.py:26
  44.2 1.6 %fusion.37 = bf16[1536,128]{0,1:T(8,128)(2,1)S(1)} fusion(bf16[1,1536,1536]{2,1,0:T(8,128)(2,1)S(1)} %bitcast.120, bf16[1536,256]{0,1:T(8,128)(2,1)S(1)} %fusion.25), kind=kOutput, calls=%fused_computation.30 | convolution fusion | flops 604176384 | bytes 5505024 | tf_op jit(solution)/shard_map/dot_general | solution.py:26
  45.8 2.1 %collective-permute-start = (bf16[1536,128]{0,1:T(8,128)(2,1)S(1)}, bf16[1536,128]{0,1:T(8,128)(2,1)S(1)}, u32[]{:S(2)}, u32[]{:S(2)}) collective-permute-start(bf16[1536,128]{0,1:T(8,128)(2,1)S(1)} %fusion.37), channel_id=1, source_target_pairs={{0,16},{16,0},{1,17},{17,1},{2,18},{18,2},{3,19},{19,3},{4,20},{20... | collective-permute-start | bytes 1179656 | tf_op jit(solution)/shard_map/ppermute | solution.py:30
  47.9 3.9 %fusion.1 = bf16[1,1536,1536]{2,1,0:T(8,128)(2,1)} fusion(f32[1536,256]{0,1:T(8,128)S(1)} %fusion.22, bf16[1536,128]{1,0:T(8,128)(2,1)S(1)} %bitcast.136, bf16[1536,128]{1,0:T(8,128)(2,1)S(1)} %bitcast.134), kind=kOutput, calls=%fused_computation.3 | convolution fusion | flops 1215430656 | bytes 7077888 | tf_op jit(solution)/shard_map/dot_general | solution.py:26
  51.8 0.0 collective-permute-done.2
  51.8 5.2 %collective-permute-done = bf16[1536,128]{0,1:T(8,128)(2,1)S(1)} collective-permute-done((bf16[1536,128]{0,1:T(8,128)(2,1)S(1)}, bf16[1536,128]{0,1:T(8,128)(2,1)S(1)}, u32[]{:S(2)}, u32[]{:S(2)}) %collective-permute-start) | collective-permute-done | bytes 393248 | tf_op jit(solution)/shard_map/ppermute | solution.py:30
  57.0 4.0 %add_convert_fusion = bf16[1536,128]{0,1:T(8,128)(2,1)S(1)} fusion(bf16[1536,128]{0,1:T(8,128)(2,1)S(1)} %collective-permute-done, bf16[1,1536,1536]{2,1,0:T(8,128)(2,1)} %param.14, bf16[1536,256]{0,1:T(8,128)(2,1)S(1)} %fusion.25), kind=kOutput, calls=%fused_computation.55 | convolution fusion | flops 604569600 | bytes 5898240 | tf_op jit(solution)/shard_map/dot_general | solution.py:26
  61.0 0.9 copy.14
  61.9 7.8 %all-to-all-start = ((bf16[16,96,128]{2,1,0:T(8,128)(2,1)}), bf16[16,96,128]{2,1,0:T(8,128)(2,1)}, u32[]{:S(2)}, u32[]{:S(2)}) async-start(bf16[16,96,128]{2,1,0:T(8,128)(2,1)} %bitcast.22), calls=%async_computation | async-start | bytes 786432 | tf_op jit(solution)/shard_map/all_to_all | solution.py:270
  69.7 0.1 slice_dynamic-update-slice_fusion.3
  69.9 0.1 slice_dynamic-update-slice_fusion.2
  70.0 0.1 slice_dynamic-update-slice_fusion.1
  70.2 0.1 slice_dynamic-update-slice_fusion
  70.3 4.6 %fusion = bf16[1,1536,1536]{2,1,0:T(8,128)(2,1)} fusion(bf16[1536,256]{0,1:T(8,128)(2,1)S(1)} %fusion.25, bf16[1536,128]{1,0:T(8,128)(2,1)S(1)} %bitcast.130, bf16[1536,128]{1,0:T(8,128)(2,1)} %bitcast.132), kind=kOutput, calls=%fused_computation.2 | convolution fusion | flops 1211891712 | bytes 6291456 | tf_op jit(solution)/shard_map/dot_general | solution.py:26
  74.9 7.1 %all-to-all-done = bf16[16,96,128]{2,1,0:T(8,128)(2,1)} async-done(((bf16[16,96,128]{2,1,0:T(8,128)(2,1)}), bf16[16,96,128]{2,1,0:T(8,128)(2,1)}, u32[]{:S(2)}, u32[]{:S(2)}) %all-to-all-start) | async-done | bytes 393248 | tf_op jit(solution)/shard_map/all_to_all | solution.py:270
  82.0 2.0 %fusion.86 = (bf16[96,512]{1,0:T(8,128)(2,1)S(1)}, f32[96,512]{1,0:T(8,128)S(1)}) fusion(bf16[96,512]{1,0:T(8,128)(2,1)S(1)} %copy-done.4, s32[512]{0:T(512)S(1)} %bitcast.144, s32[512]{0:T(512)S(1)} %bitcast.141, bf16[96,512]{1,0:T(8,128)(2,1)S(1)} %copy-done.3, bf16[16,96,128]{2,1,0:T(8,128)(2,1)} %all-to-all-done), kind=kOutput, calls=%fused_computation.95 | convolution fusion | flops 210796544 | bytes 888832 | tf_op jit(solution)/shard_map/dot_general | solution.py:26
  84.0 26.8 %shard_map.112 = bf16[16,96,512]{2,1,0:T(8,128)(2,1)S(1)} custom-call(bf16[96,512]{1,0:T(8,128)(2,1)S(1)} %get-tuple-element.26.cells), custom_call_target="tpu_custom_call" | custom-call | tf_op jit(solution)/shard_map/pallas_call | solution.py:120
  110.9 0.1 fusion.120
  111.0 0.0 copy-done
  111.0 0.5 convolution_bitcast_fusion
  111.5 0.5 convolution_bitcast_fusion.1
  112.1 0.6 fusion.60
  112.7 0.2 pad_maximum_fusion
  112.9 0.5 fusion.66
  113.4 0.2 collective-permute-start.1
  113.5 1.7 %convolution_add_fusion = f32[480,768]{1,0:T(8,128)} fusion(f32[480,768]{1,0:T(8,128)S(1)} %fusion.60, bf16[768,512]{1,0:T(8,128)(2,1)S(1)} %bitcast.123, bf16[480,1024]{1,0:T(8,128)(2,1)S(1)} %slice_dynamic-update-slice_fusion), kind=kOutput, calls=%fused_computation.44 | convolution fusion | flops 377856000 | bytes 4227072 | tf_op jit(solution)/shard_map/dot_general | solution.py:26
  115.2 3.3 %collective-permute-done.1 = bf16[96,512]{1,0:T(8,128)(2,1)S(1)} collective-permute-done((bf16[96,512]{1,0:T(8,128)(2,1)S(1)}, bf16[96,512]{1,0:T(8,128)(2,1)S(1)}, u32[]{:S(2)}, u32[]{:S(2)}) %collective-permute-start.1) | collective-permute-done | bytes 98336 | tf_op jit(solution)/shard_map/ppermute | solution.py:30
  118.5 0.7 add_convert_fusion.1
  (9 shorter events, 0.1 us)
Async XLA Ops:
  0.6 110.3 %copy-start = (bf16[5,96,768]{2,1,0:T(8,128)(2,1)S(1)}, bf16[5,96,768]{2,1,0:T(8,128)(2,1)}, u32[]{:S(2)}) copy-start(bf16[5,96,768]{2,1,0:T(8,128)(2,1)} %param.11) | copy-start | bytes 2211844
  0.6 51.1 %collective-permute-start.2 = (bf16[96,512]{1,0:T(8,128)(2,1)}, bf16[96,512]{1,0:T(8,128)(2,1)S(1)}, u32[]{:S(2)}, u32[]{:S(2)}) collective-permute-start(bf16[96,512]{1,0:T(8,128)(2,1)} %param.8), channel_id=1, source_target_pairs={{0,16},{16,0},{1,17},{17,1},{2,18},{18,2},{3,19},{19,3},{4,20},{20... | collective-permute-start | bytes 294920 | tf_op jit(solution)/shard_map/ppermute | solution.py:30
  6.2 1.7 %copy-start.2 = (bf16[96,512]{1,0:T(8,128)(2,1)S(1)}, bf16[96,512]{1,0:T(8,128)(2,1)}, u32[]{:S(2)}) copy-start(bf16[96,512]{1,0:T(8,128)(2,1)} %param.8) | copy-start | bytes 294916
  6.2 1.7 %copy-start.4 = (bf16[96,512]{1,0:T(8,128)(2,1)S(1)}, bf16[96,512]{1,0:T(8,128)(2,1)}, u32[]{:S(2)}) copy-start(bf16[96,512]{1,0:T(8,128)(2,1)} %param.9) | copy-start | bytes 294916
  8.0 1.3 %copy-start.3 = (bf16[96,512]{1,0:T(8,128)(2,1)S(1)}, bf16[96,512]{1,0:T(8,128)(2,1)}, u32[]{:S(2)}) copy-start(bf16[96,512]{1,0:T(8,128)(2,1)} %param.10) | copy-start | bytes 294916
  9.3 30.5 %slice-start = ((s8[4718592]{0:T(1024)(128)(4,1)}), s8[4194304]{0:T(1024)(128)(4,1)S(1)}, s32[]{:S(2)}) async-start(s8[4718592]{0:T(1024)(128)(4,1)} %bitcast.119), calls=%async_computation.1 | async-start | bytes 8388608
  10.7 29.1 %slice-start.1 = ((s8[4718592]{0:T(1024)(128)(4,1)}), s8[524288]{0:T(1024)(128)(4,1)S(1)}, s32[]{:S(2)}) async-start(s8[4718592]{0:T(1024)(128)(4,1)} %bitcast.119), calls=%async_computation.2 | async-start | bytes 1048576
  39.7 2.3 %slice-start.2 = ((s8[4718592]{0:T(1024)(128)(4,1)}), s8[4194304]{0:T(1024)(128)(4,1)S(1)}, s32[]{:S(2)}) async-start(s8[4718592]{0:T(1024)(128)(4,1)} %bitcast.152), calls=%async_computation.3 | async-start | bytes 8388608
  39.8 1.5 %copy-start.1 = (bf16[1,16,96,128]{3,2,1,0:T(8,128)(2,1)}, bf16[1,16,96,128]{3,2,1,0:T(8,128)(2,1)S(1)}, u32[]{:S(2)}) copy-start(bf16[1,16,96,128]{3,2,1,0:T(8,128)(2,1)S(1)} %get-tuple-element.14) | copy-start | bytes 1179652
  39.8 2.3 %slice-start.3 = ((s8[4718592]{0:T(1024)(128)(4,1)}), s8[524288]{0:T(1024)(128)(4,1)S(1)}, s32[]{:S(2)}) async-start(s8[4718592]{0:T(1024)(128)(4,1)} %bitcast.152), calls=%async_computation.4 | async-start | bytes 1048576
  45.8 11.2 %collective-permute-start = (bf16[1536,128]{0,1:T(8,128)(2,1)S(1)}, bf16[1536,128]{0,1:T(8,128)(2,1)S(1)}, u32[]{:S(2)}, u32[]{:S(2)}) collective-permute-start(bf16[1536,128]{0,1:T(8,128)(2,1)S(1)} %fusion.37), channel_id=1, source_target_pairs={{0,16},{16,0},{1,17},{17,1},{2,18},{18,2},{3,19},{19,3},{4,20},{20... | collective-permute-start | bytes 1179656 | tf_op jit(solution)/shard_map/ppermute | solution.py:30
  61.9 20.1 %all-to-all-start = ((bf16[16,96,128]{2,1,0:T(8,128)(2,1)}), bf16[16,96,128]{2,1,0:T(8,128)(2,1)}, u32[]{:S(2)}, u32[]{:S(2)}) async-start(bf16[16,96,128]{2,1,0:T(8,128)(2,1)} %bitcast.22), calls=%async_computation | async-start | bytes 786432 | tf_op jit(solution)/shard_map/all_to_all | solution.py:270
  113.4 5.1 %collective-permute-start.1 = (bf16[96,512]{1,0:T(8,128)(2,1)S(1)}, bf16[96,512]{1,0:T(8,128)(2,1)S(1)}, u32[]{:S(2)}, u32[]{:S(2)}) collective-permute-start(bf16[96,512]{1,0:T(8,128)(2,1)S(1)} %select_convert_fusion), channel_id=1, source_target_pairs={{0,16},{16,0},{1,17},{17,1},{2,18},{18,2},{3,19},{19,3},{4,20},{20... | collective-permute-start | bytes 294920 | tf_op jit(solution)/shard_map/ppermute | solution.py:30
